TPU v7x, 32 devices: a whole 2x2x4 slice. The times are simulated.
32 devices in a mesh: rows: 8 (over y, x, core), cols: 4 (over z).
Axes of the slice: x: 2, y: 2, z: 4, core: 2. Of those that a mesh axis runs over, the one named last changes fastest.
Arguments:
- tiles: bfloat16 [1024, 256, 256], P(('rows', 'cols')), may hold values from -15 to 20
- send_slot: int32 [32, 32], P(('rows', 'cols')), may hold values from 0 to 31, each once within a row
- slot_row: int32 [32, 32], P(('rows', 'cols')), may hold values from 0 to 2, as said below
- slot_fetch: int32 [32, 32], P(('rows', 'cols')), may hold values from 0 to 7
- fetch_list: int32 [32, 8], P(('rows', 'cols')), may hold values from 0 to 1
- basis: bfloat16 [16384, 128], P(('rows', 'cols')), may hold values from -6 to 6
Outputs:
- embedding: bfloat16 [16384, 128], P(('rows', 'cols'))
Inputs may be any that keep to these rules, and one draw needn't show every extreme that they name: `slot_row`: value 2 marks an empty slot. Within each block of 8 slots (one source builder) the filled slots come first; some device has all 32 slots filled in every draw.
All inputs are finite; a program needn't handle non-finite values.
Results may differ from a plain program's by a relative error of at most 0.02.
Values may be sent and summed in bfloat16 or wider, within the bound.
No kernel may reach another device: no remote copies, remote signals or barrier semaphores. Data moves between devices by JAX's collectives and lax.ppermute only.
A program may use at most 128 MiB of HBM per device.

v0:
```python
import functools

import jax
import jax.numpy as jnp
from jax import lax
from jax.experimental import pallas as pl
from jax.experimental.pallas import tpu as pltpu
from jax.sharding import PartitionSpec as P

TILE = 256
WIDTH = 128
ITERS = 6
GROUP = 8
HALF = WIDTH // 2
GROWTH = 35.0
LEAD = 3
HIGHEST = lax.Precision.HIGHEST
VMEM = pl.BlockSpec(memory_space=pltpu.VMEM)
SMEM = pl.BlockSpec(memory_space=pltpu.SMEM)
ANY = pl.BlockSpec(memory_space=pl.ANY)


def params():
    return pltpu.CompilerParams(vmem_limit_bytes=32 * 1024 * 1024)


def find_inverse(send_ref, inverse):
    def note(i, carry):
        inverse[send_ref[0, i]] = i
        return carry

    lax.fori_loop(0, inverse.shape[0], note, 0)


def lead_kernel(ncols, per, send_ref, tiles_ref, sums_ref, *refs):
    stay, leads, inverse = refs[0], refs[1:-1], refs[-1]
    me = lax.axis_index("cols")
    find_inverse(send_ref, inverse)
    lane = lax.broadcasted_iota(jnp.int32, (TILE, WIDTH), 1)
    total = jnp.zeros((TILE, WIDTH), jnp.float32)
    half = per * LEAD // 8
    for d in range(ncols):
        dest = lax.rem(me + d, ncols)
        for p in range(per):
            tile = tiles_ref[inverse[dest * per + p]]
            if d == 0:
                stay[p] = tile
            elif p < half:
                leads[d - 1][p * TILE : (p + 1) * TILE, :] = tile
            pick = jnp.where(lane == d * per + p, 1.0, 0.0).astype(jnp.bfloat16)
            total = total + jnp.dot(jnp.abs(tile), pick, preferred_element_type=jnp.float32)
    flat = jnp.transpose(total)
    sums_ref[...] = flat[:per, :]
    for d in range(1, ncols):
        rest = flat[d * per : (d + 1) * per, :]
        pieces = []
        for _ in range(3):
            pieces.append(rest.astype(jnp.bfloat16).astype(jnp.float32))
            rest = rest - pieces[-1]
        pieces.append(jnp.zeros_like(rest))
        leads[d - 1][half * TILE :, :] = jnp.concatenate(pieces, axis=0).astype(jnp.bfloat16)


def lead(tiles, send_slot, ncols):
    nslots = tiles.shape[0]
    per = nslots // ncols
    res = pl.pallas_call(
        functools.partial(lead_kernel, ncols, per),
        out_shape=[
            jax.ShapeDtypeStruct((per, TILE), jnp.float32),
            jax.ShapeDtypeStruct((per, TILE, TILE), tiles.dtype),
        ]
        + [jax.ShapeDtypeStruct((per * LEAD // 8 * TILE + 4 * per, TILE), tiles.dtype)] * (ncols - 1),
        in_specs=[SMEM, VMEM],
        out_specs=[VMEM] * (1 + ncols),
        scratch_shapes=[pltpu.SMEM((nslots,), jnp.int32)],
        compiler_params=params(),
    )(send_slot, tiles)
    return res[0], res[1], res[2:]


def rest_kernel(ncols, per, send_ref, tiles_ref, after_ref, *refs):
    outs, inverse = refs[:-1], refs[-1]
    me = lax.axis_index("cols")
    find_inverse(send_ref, inverse)
    half = per * LEAD // 8
    for d in range(1, ncols):
        dest = lax.rem(me + d, ncols)
        for p in range(half, per):
            outs[d - 1][p - half] = tiles_ref[inverse[dest * per + p]]


def rest(tiles, send_slot, ncols, after):
    nslots = tiles.shape[0]
    per = nslots // ncols
    return pl.pallas_call(
        functools.partial(rest_kernel, ncols, per),
        out_shape=[jax.ShapeDtypeStruct((per - per * LEAD // 8, TILE, TILE), tiles.dtype)] * (ncols - 1),
        in_specs=[SMEM, VMEM, ANY],
        out_specs=[VMEM] * (ncols - 1),
        scratch_shapes=[pltpu.SMEM((nslots,), jnp.int32)],
        compiler_params=params(),
    )(send_slot, tiles, after)


def later_kernel(list_ref, after_ref, out_ref):
    for g in range(out_ref.shape[1]):
        out_ref[0, g] = list_ref[0, g]


def later(fetch_list, after):
    return pl.pallas_call(
        later_kernel,
        out_shape=jax.ShapeDtypeStruct(fetch_list.shape, fetch_list.dtype),
        in_specs=[SMEM, ANY],
        out_specs=SMEM,
        compiler_params=params(),
    )(fetch_list, after)


def send_blocks(scaled, wanted, outs):
    for d, out in enumerate(outs):
        out[...] = scaled[pl.ds(pl.multiple_of(wanted[d] * TILE, TILE), TILE), :]


def start_kernel(ncols, groups, blocks, row_ref, *refs):
    lists, refs = refs[:groups], refs[groups:]
    (sums_ref, *leads), (basis_ref, scale_ref, asked_ref, *outs, scaled) = refs[:ncols], refs[ncols:]
    me, row = lax.axis_index("cols"), lax.axis_index("rows")
    per = sums_ref.shape[0]
    sums = [sums_ref[...]]
    for ref in leads:
        tail = ref[per * LEAD // 8 * TILE :, :].astype(jnp.float32)
        sums.append(tail[:per, :] + tail[per : 2 * per, :] + tail[2 * per : 3 * per, :])
    degree = [jnp.ones((1, TILE), jnp.float32) for _ in range(blocks)]
    for d in range(ncols):
        source = lax.rem(me + ncols - d, ncols)
        for p in range(per):
            at = row_ref[0, source * per + p]
            line = sums[d][p : p + 1, :]
            for j in range(blocks):
                degree[j] = degree[j] + jnp.where(at == j, line, jnp.zeros_like(line))
    for j in range(blocks):
        here = slice(j * TILE, (j + 1) * TILE)
        scale = jnp.transpose(jnp.broadcast_to(lax.rsqrt(degree[j]), (WIDTH, TILE)))
        scale_ref[here, :] = scale
        scaled[here, :] = (scale * basis_ref[here, :].astype(jnp.float32)).astype(jnp.bfloat16)
    wanted = [lists[d][0, row] for d in range(groups)]
    for d in range(groups):
        asked_ref[0, d] = wanted[d]
    send_blocks(scaled, wanted, outs)


def start(slot_row, lists, sums, basis):
    ncols, groups, rows = len(sums), len(lists), basis.shape[0]
    res = pl.pallas_call(
        functools.partial(start_kernel, ncols, groups, rows // TILE),
        out_shape=[
            jax.ShapeDtypeStruct((rows, WIDTH), jnp.float32),
            jax.ShapeDtypeStruct((1, groups), jnp.int32),
        ]
        + [jax.ShapeDtypeStruct((TILE, WIDTH), jnp.bfloat16)] * groups,
        in_specs=[SMEM] * (1 + groups) + [VMEM] * (ncols + 1),
        out_specs=[VMEM, SMEM] + [VMEM] * groups,
        scratch_shapes=[pltpu.VMEM((rows, WIDTH), jnp.bfloat16)],
        compiler_params=params(),
    )(slot_row, *lists, *sums, basis)
    return res[0], res[1], res[2:]


def gram_of(y):
    return lax.dot_general(
        y, y, (((0,), (0,)), ((), ())), precision=HIGHEST, preferred_element_type=jnp.float32
    )


def times(a, b, transposed=False):
    return lax.dot_general(
        a, b, (((1,), (1 if transposed else 0,)), ((), ())), precision=HIGHEST, preferred_element_type=jnp.float32
    )


def step_kernel(ncols, groups, first, last, row_ref, fetch_ref, asked_ref, scale_ref, *refs):
    stay, leads, rests, refs = refs[0], refs[1:ncols], refs[ncols : 2 * ncols - 1], refs[2 * ncols - 1 :]
    got, refs = refs[:groups], refs[groups:]
    outs, (held, acc, scaled) = refs[:-3], refs[-3:]
    me, row = lax.axis_index("cols"), lax.axis_index("rows")
    per, rows = stay.shape[0], scale_ref.shape[0]
    half = per * LEAD // 8
    for d in range(groups):
        held[d] = got[d][...]
    acc[...] = jnp.zeros_like(acc)
    for d in range(ncols):
        source = lax.rem(me + ncols - d, ncols)
        for p in range(per):
            slot = source * per + p
            which = jnp.bitwise_xor(fetch_ref[0, slot], row)
            place = pl.ds(pl.multiple_of(row_ref[0, slot] * TILE, TILE), TILE)
            if d == 0:
                tile = stay[p]
            elif p < half:
                tile = leads[d - 1][p * TILE : (p + 1) * TILE, :]
            else:
                tile = rests[d - 1][p - half]
            acc[place, :] += jnp.dot(tile, held[which], preferred_element_type=jnp.float32)
    scale = scale_ref[...]
    y = acc[:rows, :] * scale
    if last:
        outs[0][...] = y
        return
    gram_ref, outs = outs[0], outs[1:]
    gram_ref[:HALF, :], gram_ref[HALF:, :] = fold(gram_of(y))
    if first:
        scaled[...] = (y * scale).astype(jnp.bfloat16)
        send_blocks(scaled, [asked_ref[0, d] for d in range(groups)], outs)
    else:
        outs[0][...] = y


def step(slot_row, slot_fetch, asked, scale, chunks, got, first, last):
    ncols, groups, rows = (len(chunks) + 1) // 2, len(got), scale.shape[0]
    shapes = [] if last else [jax.ShapeDtypeStruct((HALF + 8, WIDTH), jnp.float32)]
    if first:
        shapes += [jax.ShapeDtypeStruct((TILE, WIDTH), jnp.bfloat16)] * groups
    else:
        shapes += [jax.ShapeDtypeStruct((rows, WIDTH), jnp.float32)]
    res = pl.pallas_call(
        functools.partial(step_kernel, ncols, groups, first, last),
        out_shape=shapes,
        in_specs=[SMEM] * 3 + [VMEM] * (1 + len(chunks) + groups),
        out_specs=[VMEM] * len(shapes),
        scratch_shapes=[
            pltpu.VMEM((groups, TILE, WIDTH), jnp.bfloat16),
            pltpu.VMEM((rows + TILE, WIDTH), jnp.float32),
            pltpu.VMEM((rows, WIDTH), jnp.bfloat16),
        ],
        compiler_params=params(),
    )(slot_row, slot_fetch, asked, scale, *chunks, *got)
    if last:
        return None, res[0]
    return res[0], (res[1:] if first else res[1])


def added(parts):
    while len(parts) > 1:
        parts = [parts[i] + parts[i + 1] for i in range(0, len(parts), 2)]
    return parts[0]


def summed(refs):
    return added([ref[...] for ref in refs])


def turn_kernel(npts, groups, nparts, first, last, gauge, asked_ref, scale_ref, p_ref, *refs):
    parts, refs = refs[:nparts], refs[nparts:]
    if not first:
        before_ref, before_inv_ref, refs = refs[0], refs[1], refs[2:]
    outs, (inv, scaled) = refs[:-2], refs[-2:]
    gram = unfold(summed(parts)) * (1.0 / npts)
    factor_rows(gram, inv)
    both = inv[...]
    mine = both if first else times(both, before_ref[...])
    y = times(p_ref[...], mine, True)
    if last:
        gram_ref, y_ref = outs
        y_ref[...] = y
        gram_ref[:HALF, :], gram_ref[HALF:, :] = fold(gram_of(y))
        return
    low_ref, inv_ref, growth_ref, outs = outs[0], outs[1], outs[2], outs[3:]
    scaled[...] = (y * scale_ref[...]).astype(jnp.bfloat16)
    send_blocks(scaled, [asked_ref[0, d] for d in range(groups)], outs)
    low = times(gram, both, True)
    low = low if first else times(before_inv_ref[...], low)
    low_ref[...] = low
    inv_ref[...] = mine
    if not gauge:
        return
    weights = lax.dot_general(
        jnp.ones((8, WIDTH), jnp.float32), low * low, (((1,), (1,)), ((), ())), preferred_element_type=jnp.float32
    )
    growth = jnp.sum(mine * mine * weights[0:1, :]) * (1.0 / WIDTH)
    growth_ref[...] = jnp.full((8, WIDTH), growth)


def turn(asked, parts, scale, p, before, npts, last, gauge):
    rows, groups = p.shape[0], asked.shape[1]
    first = before is None
    square = jax.ShapeDtypeStruct((WIDTH, WIDTH), jnp.float32)
    growth = jax.ShapeDtypeStruct((8, WIDTH), jnp.float32)
    if last:
        shapes = [jax.ShapeDtypeStruct((HALF + 8, WIDTH), jnp.float32), jax.ShapeDtypeStruct(p.shape, p.dtype)]
    else:
        shapes = [square, square, growth] + [jax.ShapeDtypeStruct((TILE, WIDTH), jnp.bfloat16)] * groups
    return pl.pallas_call(
        functools.partial(turn_kernel, npts, groups, len(parts), first, last, gauge),
        out_shape=shapes,
        in_specs=[SMEM] + [VMEM] * (2 + len(parts) + (0 if first else 2)),
        out_specs=[VMEM] * len(shapes),
        scratch_shapes=[pltpu.VMEM((WIDTH, WIDTH), jnp.float32), pltpu.VMEM((rows, WIDTH), jnp.bfloat16)],
        compiler_params=params(),
    )(asked, scale, p, *parts, *([] if first else before))


def careful_kernel(npts, groups, nparts, asked_ref, scale_ref, y_ref, *refs):
    parts, (v_ref, *outs), (inv, scaled) = refs[:nparts], refs[nparts:-2], refs[-2:]
    factor_rows(unfold(summed(parts)) * (1.0 / npts), inv)
    v = times(y_ref[...], inv[...], True).astype(jnp.bfloat16)
    v_ref[...] = v
    scaled[...] = (v.astype(jnp.float32) * scale_ref[...]).astype(jnp.bfloat16)
    send_blocks(scaled, [asked_ref[0, d] for d in range(groups)], outs)


def careful(asked, parts, scale, y, npts):
    rows, groups = y.shape[0], asked.shape[1]
    res = pl.pallas_call(
        functools.partial(careful_kernel, npts, groups, len(parts)),
        out_shape=[jax.ShapeDtypeStruct(y.shape, jnp.bfloat16)]
        + [jax.ShapeDtypeStruct((TILE, WIDTH), jnp.bfloat16)] * groups,
        in_specs=[SMEM] + [VMEM] * (2 + len(parts)),
        out_specs=[VMEM] * (1 + groups),
        scratch_shapes=[pltpu.VMEM((WIDTH, WIDTH), jnp.float32), pltpu.VMEM((rows, WIDTH), jnp.bfloat16)],
        compiler_params=params(),
    )(asked, scale, y, *parts)
    return res[0], res[1:]


def fold(square):
    row = lax.broadcasted_iota(jnp.int32, (HALF, WIDTH), 0)
    lane = lax.broadcasted_iota(jnp.int32, (HALF, WIDTH), 1)
    low = square[HALF:, :]
    moved = pltpu.roll(low, HALF, 1)
    main = jnp.where((lane < HALF) & (lane > row), moved, square[:HALF, :])
    diagonal = jnp.sum(jnp.where(lane == row + HALF, low, 0.0), axis=0, keepdims=True)
    return main, jnp.broadcast_to(diagonal, (8, WIDTH))


def unfold(folded):
    row = lax.broadcasted_iota(jnp.int32, (HALF, WIDTH), 0)
    lane = lax.broadcasted_iota(jnp.int32, (HALF, WIDTH), 1)
    main = folded[:HALF, :]
    diagonal = jnp.broadcast_to(folded[HALF : HALF + 1, :], (HALF, WIDTH))
    upper = jnp.where((lane >= HALF) | (lane <= row), main, 0.0)
    moved = pltpu.roll(main, HALF, 1)
    lower = jnp.where(lane > row + HALF, moved, jnp.where(lane == row + HALF, diagonal, 0.0))
    whole = jnp.concatenate([upper, lower], axis=0)
    row = lax.broadcasted_iota(jnp.int32, (WIDTH, WIDTH), 0)
    lane = lax.broadcasted_iota(jnp.int32, (WIDTH, WIDTH), 1)
    return jnp.where(row == lane, whole, whole + jnp.transpose(whole))


def factor_rows(matrix, out_ref):
    n = WIDTH
    lane = lax.broadcasted_iota(jnp.int32, (8, n), 1)
    parts = [matrix[8 * i : 8 * i + 8, :] for i in range(n // 8)]
    for j in range(0, n, GROUP):
        here = j // 8
        off = j % 8
        wide = lambda v: jnp.broadcast_to(v, (8, n))
        rows = [wide(parts[here][off + a : off + a + 1, :]) for a in range(GROUP)]
        piv = [[wide(rows[a][:, j + c : j + c + 1]) for c in range(a + 1)] for a in range(GROUP)]
        in_group = (lane >= j) & (lane < j + GROUP)
        rows = [jnp.where(in_group, jnp.where(lane == j + a, 1.0, 0.0), rows[a]) for a in range(GROUP)]
        low = [[None] * GROUP for _ in range(GROUP)]
        inv = []
        for c in range(GROUP):
            inv.append(1.0 / piv[c][c])
            for a in range(c + 1, GROUP):
                low[a][c] = piv[a][c] * inv[c]
            for a in range(c + 1, GROUP):
                for b in range(c + 1, a + 1):
                    piv[a][b] = piv[a][b] - low[a][c] * piv[b][c]
        for a in range(GROUP):
            for c in range(a):
                rows[a] = rows[a] - low[a][c] * rows[c]
        for a in range(GROUP):
            keep = jnp.where(lane <= j + a, rows[a], 0.0) * lax.rsqrt(piv[a][a])
            out_ref[j + a : j + a + 1, :] = keep[0:1, :]
        scaled = [rows[a] * inv[a] for a in range(GROUP)]
        for i in range(here + 1, n // 8):
            cols = [wide(parts[i][:, j + c : j + c + 1]) for c in range(GROUP)]
            new = jnp.where(in_group, 0.0, parts[i])
            for c in range(GROUP):
                for b in range(c):
                    cols[c] = cols[c] - low[c][b] * cols[b]
                new = new - cols[c] * scaled[c]
            parts[i] = new


def finish_kernel(npts, nparts, y_ref, *refs):
    v_ref, inv = refs[nparts:]
    factor_rows(unfold(summed(refs[:nparts])) * (1.0 / npts), inv)
    v_ref[...] = times(y_ref[...], inv[...], True).astype(v_ref.dtype)


def finish(parts, y, npts):
    return pl.pallas_call(
        functools.partial(finish_kernel, npts, len(parts)),
        out_shape=jax.ShapeDtypeStruct(y.shape, jnp.bfloat16),
        in_specs=[VMEM] * (1 + len(parts)),
        out_specs=VMEM,
        scratch_shapes=[pltpu.VMEM((WIDTH, WIDTH), jnp.float32)],
        compiler_params=params(),
    )(y, *parts)


def swap(x, axis, n, d):
    return lax.ppermute(x, axis, [(i, i ^ d) for i in range(n)])


def shift(x, axis, n, d):
    return lax.ppermute(x, axis, [(i, (i + d) % n) for i in range(n)])


def on_device(tiles, send_slot, slot_row, slot_fetch, fetch_list, basis):
    groups = lax.axis_size("rows")
    ncols = lax.axis_size("cols")
    npts = basis.shape[0] * groups * ncols
    sums, stay, leads = lead(tiles, send_slot, ncols)
    rests = rest(tiles, send_slot, ncols, leads[0])
    wish = later(fetch_list, rests[0])
    leads = [shift(leads[d - 1], "cols", ncols, d) for d in range(1, ncols)]
    rests = [shift(rests[d - 1], "cols", ncols, d) for d in range(1, ncols)]
    chunks = [stay, *leads, *rests]
    lists = [wish] + [swap(wish, "rows", groups, d) for d in range(1, groups)]
    scale, asked, out = start(slot_row, lists, [sums, *leads], basis)
    stages = [("rows", groups, [1])]
    bit = 2
    while bit < groups:
        wide = bit * 2 < groups
        stages.append(("rows", groups, [bit, 2 * bit, 3 * bit] if wide else [bit]))
        bit *= 4 if wide else 2
    apart = [("cols", ncols, [1 << i]) for i in range(ncols.bit_length() - 1)]
    at_once = [("cols", ncols, list(range(1, ncols)))]

    def total(gram, more):
        for axis, size, partners in stages + more:
            parts = [gram] + [swap(gram, axis, size, d) for d in partners]
            gram = added(parts)
        return parts

    def fetched(out):
        return [out[0]] + [swap(out[d], "rows", groups, d) for d in range(1, groups)]

    first_out, growth = out, []
    parts = before = None
    for k in range(ITERS):
        last = k == ITERS - 1
        gram, out = step(slot_row, slot_fetch, asked, scale, chunks, fetched(out), k == 0, last)
        if k:
            gauge = k in (2, ITERS - 2)
            res = turn(asked, parts, scale, out, before, npts, last, gauge)
            before, out = res[:2], res[3:]
            if gauge:
                growth.append(res[2][0, 0])
        if not last:
            parts = total(gram, apart)
    gram, y = res
    fast = finish(total(gram, at_once), y, npts)

    def repeat(k, state):
        gram, y = step(slot_row, slot_fetch, asked, scale, chunks, fetched(state[1]), False, False)
        v, out = careful(asked, total(gram, apart), scale, y, npts)
        return v, tuple(out)

    return lax.cond(
        sum(growth) < GROWTH,
        lambda: fast,
        lambda: lax.fori_loop(0, ITERS, repeat, (fast, tuple(first_out)))[0],
    )


def solution(mesh):
    in_specs = (
        P(("rows", "cols"), None, None),
        P(("rows", "cols"), None),
        P(("rows", "cols"), None),
        P(("rows", "cols"), None),
        P(("rows", "cols"), None),
        P(("rows", "cols"), None),
    )
    out_specs = P(("rows", "cols"), None)
    return jax.shard_map(
        on_device, mesh=mesh, in_specs=in_specs, out_specs=out_specs, check_vma=False
    )
```

profile of v0, /device:TPU:0, one launch (start us, length us, event | category | flops | bytes accessed | tf_op | source)
XLA Modules:
  0.0 258.5 jit_solution(10977550618101155007)
XLA Ops:
  0.0 2.2 copy-done
  2.9 2.2 shard_map.66
  5.0 3.1 %collective-permute-start.20 = (bf16[800,256]{1,0:T(8,128)(2,1)S(1)}, bf16[800,256]{1,0:T(8,128)(2,1)S(1)}, u32[]{:S(2)}, u32[]{:S(2)}) collective-permute-start(bf16[800,256]{1,0:T(8,128)(2,1)S(1)} %get-tuple-element.265.after_ref), channel_id=1, source_target_pairs={{0,1},{1,2},{2,3},{3,0},{4,5},{5,6},{6,7},{7,4},{8,9},{9,10},{10,1... | collective-permute-start | bytes 1228808 | tf_op jit(solution)/shard_map/ppermute | solution.py:411
  8.1 2.6 %collective-permute-start.21 = (bf16[800,256]{1,0:T(8,128)(2,1)S(1)}, bf16[800,256]{1,0:T(8,128)(2,1)}, u32[]{:S(2)}, u32[]{:S(2)}) collective-permute-start(bf16[800,256]{1,0:T(8,128)(2,1)S(1)} %get-tuple-element.268), channel_id=1, source_target_pairs={{0,2},{1,3},{2,0},{3,1},{4,6},{5,7},{6,4},{7,5},{8,10},{9,11},{10,... | collective-permute-start | bytes 1228808 | tf_op jit(solution)/shard_map/ppermute | solution.py:411
  14.3 1.6 collective-permute-start.14
  17.9 1.5 collective-permute-start.16
  21.4 2.4 collective-permute-start.18
  24.4 1.5 collective-permute-done.18.refs_6_
  28.1 3.1 %collective-permute-start.25 = (bf16[5,256,256]{2,1,0:T(8,128)(2,1)S(1)}, bf16[5,256,256]{2,1,0:T(8,128)(2,1)}, u32[]{:S(2)}, u32[]{:S(2)}) collective-permute-start(bf16[5,256,256]{2,1,0:T(8,128)(2,1)S(1)} %get-tuple-element.274), channel_id=1, source_target_pairs={{0,3},{1,0},{2,1},{3,2},{4,7},{5,4},{6,5},{7,6},{8,11},{9,8},{10,9... | collective-permute-start | bytes 1966088 | tf_op jit(solution)/shard_map/ppermute | solution.py:411
  31.2 7.1 %collective-permute-done.21.refs_10_.refs_2_ = bf16[800,256]{1,0:T(8,128)(2,1)} collective-permute-done((bf16[800,256]{1,0:T(8,128)(2,1)S(1)}, bf16[800,256]{1,0:T(8,128)(2,1)}, u32[]{:S(2)}, u32[]{:S(2)}) %collective-permute-start.21) | collective-permute-done | bytes 409632 | tf_op jit(solution)/shard_map/ppermute | solution.py:411
  38.3 2.2 shard_map.69
  40.5 1.8 collective-permute-start.27
  43.3 2.0 collective-permute-done.27.refs_9_
  45.3 1.8 collective-permute-start.29
  48.3 1.4 collective-permute-done.29.refs_11_
  49.7 3.6 %collective-permute-start.31 = (bf16[256,128]{1,0:T(8,128)(2,1)}, bf16[256,128]{1,0:T(8,128)(2,1)S(1)}, u32[]{:S(2)}, u32[]{:S(2)}) collective-permute-start(bf16[256,128]{1,0:T(8,128)(2,1)} %get-tuple-element.281), channel_id=1, source_target_pairs={{0,24},{4,28},{8,16},{12,20},{16,8},{20,12},{24,0},{28,4},{1,25},{... | collective-permute-start | bytes 196616 | tf_op jit(solution)/shard_map/ppermute | solution.py:407
  54.0 1.9 collective-permute-done.31.refs_13_
  55.8 2.3 collective-permute-done.32.refs_14_
  58.1 30.1 %collective-permute-done.24.refs_5_ = bf16[5,256,256]{2,1,0:T(8,128)(2,1)S(1)} collective-permute-done((bf16[5,256,256]{2,1,0:T(8,128)(2,1)S(1)}, bf16[5,256,256]{2,1,0:T(8,128)(2,1)S(1)}, u32[]{:S(2)}, u32[]{:S(2)}) %collective-permute-start.24) | collective-permute-done | bytes 655392 | tf_op jit(solution)/shard_map/ppermute | solution.py:411
  88.2 3.2 %shard_map.70 = (f32[72,128]{1,0:T(8,128)S(1)}, bf16[256,128]{1,0:T(8,128)(2,1)S(1)}, bf16[256,128]{1,0:T(8,128)(2,1)S(1)}, bf16[256,128]{1,0:T(8,128)(2,1)S(1)}...) custom-call(s32[1,32]{1,0:T(1,128)S(1)} %copy-done.4, ...), custom_call_target="tpu_custom_call" | custom-call | tf_op jit(solution)/shard_map/pallas_call | solution.py:227
  92.7 1.5 collective-permute-start.42
  94.3 1.4 collective-permute-start.43
  96.2 1.5 collective-permute-start.34
  97.7 1.7 collective-permute-done.43
  100.0 14.7 %collective-permute-start.44 = (f32[72,128]{1,0:T(8,128)S(1)}, f32[72,128]{1,0:T(8,128)S(1)}, u32[]{:S(2)}, u32[]{:S(2)}) collective-permute-start(f32[72,128]{1,0:T(8,128)S(1)} %add_add_fusion.6), channel_id=1, source_target_pairs={{0,1},{1,0},{2,3},{3,2},{4,5},{5,4},{6,7},{7,6},{8,9},{9,8},{10,11... | collective-permute-start | bytes 110600 | tf_op jit(solution)/shard_map/ppermute | solution.py:407
  114.7 1.5 collective-permute-start.36
  116.8 2.3 collective-permute-start.38
  119.1 1.5 collective-permute-start.45
  120.7 2.0 collective-permute-done.37.refs_12_
  123.7 3.2 %shard_map.71 = (f32[72,128]{1,0:T(8,128)S(1)}, f32[512,128]{1,0:T(8,128)S(1)}) custom-call(s32[1,32]{1,0:T(1,128)S(1)} %copy-done.4, s32[1,32]{1,0:T(1,128)S(1)} %copy-done.5, s32[1,8]{1,0:T(1,128)S(1)} %get-tuple-element.270.asked_ref, f32[512,128]{1,0:T(8,128)S(1)} %get-tuple-element.271.scale_ref, bf16[8,256,256]{2,1,0:T(8,128)(2,1)S(1)} %get-tuple-element.272.refs_0_, ...), custom_call_target="tpu_custom_call" | custom-call | tf_op jit(solution)/shard_map/pallas_call | solution.py:227
  127.0 5.9 %shard_map.72 = (f32[128,128]{1,0:T(8,128)S(1)}, f32[128,128]{1,0:T(8,128)S(1)}, f32[8,128]{1,0:T(8,128)}, bf16[256,128]{1,0:T(8,128)(2,1)S(1)}, bf16[256,128]{1...) custom-call(s32[1,8]{1,0:T(1,128)S(1)} %get-tuple-element.270.asked_, ...), custom_call_target="tpu_custom_call" | custom-call | tf_op jit(solution)/shard_map/pallas_call | solution.py:294
  135.4 1.6 collective-permute-start.56
  138.2 2.0 collective-permute-done.56
  141.2 1.8 collective-permute-start.51
  143.0 1.7 collective-permute-start.52
  145.6 1.5 collective-permute-done.51.refs_13_
  147.9 3.4 %shard_map.73 = (f32[72,128]{1,0:T(8,128)S(1)}, f32[512,128]{1,0:T(8,128)S(1)}) custom-call(s32[1,32]{1,0:T(1,128)S(1)} %copy-done.4, s32[1,32]{1,0:T(1,128)S(1)} %copy-done.5, s32[1,8]{1,0:T(1,128)S(1)} %get-tuple-element.270.asked_ref, f32[512,128]{1,0:T(8,128)S(1)} %get-tuple-element.271.scale_ref, bf16[8,256,256]{2,1,0:T(8,128)(2,1)S(1)} %get-tuple-element.272.refs_0_, ...), custom_call_target="tpu_custom_call" | custom-call | tf_op jit(solution)/shard_map/pallas_call | solution.py:227
  152.3 1.5 collective-permute-start.58
  154.5 2.0 collective-permute-start.69
  157.4 6.3 %shard_map.74 = (f32[128,128]{1,0:T(8,128)S(1)}, f32[128,128]{1,0:T(8,128)S(1)}, f32[8,128]{1,0:T(8,128)S(1)}, bf16[256,128]{1,0:T(8,128)(2,1)S(1)}, bf16[256,12...) custom-call(s32[1,8]{1,0:T(1,128)S(1)} %get-tuple-element.270.asked_, ...), custom_call_target="tpu_custom_call" | custom-call | tf_op jit(solution)/shard_map/pallas_call | solution.py:294
  168.4 1.6 collective-permute-start.64
  170.2 1.5 collective-permute-start.71
  171.7 1.8 collective-permute-done.64.refs_13_
  173.6 1.4 collective-permute-done.65.refs_14_
  175.0 3.2 %shard_map.75 = (f32[72,128]{1,0:T(8,128)S(1)}, f32[512,128]{1,0:T(8,128)S(1)}) custom-call(s32[1,32]{1,0:T(1,128)S(1)} %copy-done.4, s32[1,32]{1,0:T(1,128)S(1)} %copy-done.5, s32[1,8]{1,0:T(1,128)S(1)} %get-tuple-element.270.asked_ref, f32[512,128]{1,0:T(8,128)S(1)} %get-tuple-element.271.scale_ref, bf16[8,256,256]{2,1,0:T(8,128)(2,1)S(1)} %get-tuple-element.272.refs_0_, ...), custom_call_target="tpu_custom_call" | custom-call | tf_op jit(solution)/shard_map/pallas_call | solution.py:227
  178.2 6.2 %shard_map.76 = (f32[128,128]{1,0:T(8,128)S(1)}, f32[128,128]{1,0:T(8,128)S(1)}, f32[8,128]{1,0:T(8,128)}, bf16[256,128]{1,0:T(8,128)(2,1)S(1)}, bf16[256,128]{1...) custom-call(s32[1,8]{1,0:T(1,128)S(1)} %get-tuple-element.270.asked_, ...), custom_call_target="tpu_custom_call" | custom-call | tf_op jit(solution)/shard_map/pallas_call | solution.py:294
  190.0 2.0 collective-permute-done.82
  193.3 1.4 collective-permute-start.77
  194.8 2.0 collective-permute-start.78
  200.3 3.2 %shard_map.77 = (f32[72,128]{1,0:T(8,128)S(1)}, f32[512,128]{1,0:T(8,128)S(1)}) custom-call(s32[1,32]{1,0:T(1,128)S(1)} %copy-done.4, s32[1,32]{1,0:T(1,128)S(1)} %copy-done.5, s32[1,8]{1,0:T(1,128)S(1)} %get-tuple-element.270.asked_ref, f32[512,128]{1,0:T(8,128)S(1)} %get-tuple-element.271.scale_ref, bf16[8,256,256]{2,1,0:T(8,128)(2,1)S(1)} %get-tuple-element.272.refs_0_, ...), custom_call_target="tpu_custom_call" | custom-call | tf_op jit(solution)/shard_map/pallas_call | solution.py:227
  204.3 1.6 collective-permute-start.84
  207.9 1.5 collective-permute-start.93
  209.4 6.3 %shard_map.78 = (f32[128,128]{1,0:T(8,128)S(1)}, f32[128,128]{1,0:T(8,128)S(1)}, f32[8,128]{1,0:T(8,128)S(1)}, bf16[256,128]{1,0:T(8,128)(2,1)S(1)}, bf16[256,12...) custom-call(s32[1,8]{1,0:T(1,128)S(1)} %get-tuple-element.270.asked_, ...), custom_call_target="tpu_custom_call" | custom-call | tf_op jit(solution)/shard_map/pallas_call | solution.py:294
  216.6 1.5 collective-permute-start.96
  219.0 1.5 collective-permute-start.89
  220.4 1.4 collective-permute-start.90
  222.9 1.5 collective-permute-start.97
  225.7 1.4 collective-permute-done.91.refs_14_
  227.1 2.7 %shard_map.79.p_ref = f32[512,128]{1,0:T(8,128)S(1)} custom-call(s32[1,32]{1,0:T(1,128)S(1)} %copy-done.4, s32[1,32]{1,0:T(1,128)S(1)} %copy-done.5, s32[1,8]{1,0:T(1,128)S(1)} %get-tuple-element.270.asked_ref, f32[512,128]{1,0:T(8,128)S(1)} %get-tuple-element.271.scale_ref, bf16[8,256,256]{2,1,0:T(8,128)(2,1)S(1)} %get-tuple-element.272.refs_0_, ...), custom_call_target="tpu_custom_call" | custom-call | tf_op jit(solution)/shard_map/pallas_call | solution.py:227
  229.8 6.8 %shard_map.80 = (f32[72,128]{1,0:T(8,128)S(1)}, f32[512,128]{1,0:T(8,128)S(1)}) custom-call(s32[1,8]{1,0:T(1,128)S(1)} %get-tuple-element.270.asked_ref, f32[512,128]{1,0:T(8,128)S(1)} %get-tuple-element.271.scale_ref, f32[512,128]{1,0:T(8,128)S(1)} %shard_map.79.p_ref, f32[72,128]{1,0:T(8,128)S(1)} %add.134.refs_0_, ...), custom_call_target="tpu_custom_call" | custom-call | tf_op jit(solution)/shard_map/pallas_call | solution.py:294
  241.9 2.1 collective-permute-done.101
  246.8 1.9 collective-permute-start.104
  251.1 1.5 collective-permute-done.104.refs_3_
  252.6 5.7 %shard_map.81 = bf16[512,128]{1,0:T(8,128)(2,1)} custom-call(f32[512,128]{1,0:T(8,128)S(1)} %get-tuple-element.342.y_ref, f32[72,128]{1,0:T(8,128)S(1)} %add_add_fusion.1.refs_0_, f32[72,128]{1,0:T(8,128)S(1)} %collective-permute-done.102.refs_1_, f32[72,128]{1,0:T(8,128)S(1)} %collective-permute-done.103.refs_2_, f32[72,128]{1,0:T(8,128)S(1)} %collective-permute-done.104.refs_3_), custom_call_target="tpu_custom_call" | custom-call | tf_op jit(solution)/shard_map/pallas_call | solution.py:396
  (168 shorter events, 58.5 us)
Async XLA Ops:
  5.0 23.0 %collective-permute-start.20 = (bf16[800,256]{1,0:T(8,128)(2,1)S(1)}, bf16[800,256]{1,0:T(8,128)(2,1)S(1)}, u32[]{:S(2)}, u32[]{:S(2)}) collective-permute-start(bf16[800,256]{1,0:T(8,128)(2,1)S(1)} %get-tuple-element.265.after_ref), channel_id=1, source_target_pairs={{0,1},{1,2},{2,3},{3,0},{4,5},{5,6},{6,7},{7,4},{8,9},{9,10},{10,1... | collective-permute-start | bytes 1228808 | tf_op jit(solution)/shard_map/ppermute | solution.py:411
  8.1 30.2 %collective-permute-start.21 = (bf16[800,256]{1,0:T(8,128)(2,1)S(1)}, bf16[800,256]{1,0:T(8,128)(2,1)}, u32[]{:S(2)}, u32[]{:S(2)}) collective-permute-start(bf16[800,256]{1,0:T(8,128)(2,1)S(1)} %get-tuple-element.268), channel_id=1, source_target_pairs={{0,2},{1,3},{2,0},{3,1},{4,6},{5,7},{6,4},{7,5},{8,10},{9,11},{10,... | collective-permute-start | bytes 1228808 | tf_op jit(solution)/shard_map/ppermute | solution.py:411
  10.7 27.6 %collective-permute-start.22 = (bf16[800,256]{1,0:T(8,128)(2,1)S(1)}, bf16[800,256]{1,0:T(8,128)(2,1)}, u32[]{:S(2)}, u32[]{:S(2)}) collective-permute-start(bf16[800,256]{1,0:T(8,128)(2,1)S(1)} %get-tuple-element.269), channel_id=1, source_target_pairs={{0,3},{1,0},{2,1},{3,2},{4,7},{5,4},{6,5},{7,6},{8,11},{9,8},{10,9... | collective-permute-start | bytes 1228808 | tf_op jit(solution)/shard_map/ppermute | solution.py:411
  25.9 32.3 %collective-permute-start.23 = (bf16[5,256,256]{2,1,0:T(8,128)(2,1)S(1)}, bf16[5,256,256]{2,1,0:T(8,128)(2,1)S(1)}, u32[]{:S(2)}, u32[]{:S(2)}) collective-permute-start(bf16[5,256,256]{2,1,0:T(8,128)(2,1)S(1)} %get-tuple-element.266.after_ref), channel_id=1, source_target_pairs={{0,1},{1,2},{2,3},{3,0},{4,5},{5,6},{6,7},{7,4},{8,9},{9,10},{10,1... | collective-permute-start | bytes 1966088 | tf_op jit(solution)/shard_map/ppermute | solution.py:411
  27.7 60.5 %collective-permute-start.24 = (bf16[5,256,256]{2,1,0:T(8,128)(2,1)S(1)}, bf16[5,256,256]{2,1,0:T(8,128)(2,1)S(1)}, u32[]{:S(2)}, u32[]{:S(2)}) collective-permute-start(bf16[5,256,256]{2,1,0:T(8,128)(2,1)S(1)} %get-tuple-element.273), channel_id=1, source_target_pairs={{0,2},{1,3},{2,0},{3,1},{4,6},{5,7},{6,4},{7,5},{8,10},{9,11},{10,... | collective-permute-start | bytes 1966088 | tf_op jit(solution)/shard_map/ppermute | solution.py:411
  28.1 60.2 %collective-permute-start.25 = (bf16[5,256,256]{2,1,0:T(8,128)(2,1)S(1)}, bf16[5,256,256]{2,1,0:T(8,128)(2,1)}, u32[]{:S(2)}, u32[]{:S(2)}) collective-permute-start(bf16[5,256,256]{2,1,0:T(8,128)(2,1)S(1)} %get-tuple-element.274), channel_id=1, source_target_pairs={{0,3},{1,0},{2,1},{3,2},{4,7},{5,4},{6,5},{7,6},{8,11},{9,8},{10,9... | collective-permute-start | bytes 1966088 | tf_op jit(solution)/shard_map/ppermute | solution.py:411
  40.5 4.7 %collective-permute-start.27 = (bf16[256,128]{1,0:T(8,128)(2,1)}, bf16[256,128]{1,0:T(8,128)(2,1)S(1)}, u32[]{:S(2)}, u32[]{:S(2)}) collective-permute-start(bf16[256,128]{1,0:T(8,128)(2,1)} %get-tuple-element.277), channel_id=1, source_target_pairs={{0,8},{4,12},{8,0},{12,4},{16,24},{20,28},{24,16},{28,20},{1,9},{5... | collective-permute-start | bytes 196616 | tf_op jit(solution)/shard_map/ppermute | solution.py:407
  47.0 6.3 %collective-permute-start.30 = (bf16[256,128]{1,0:T(8,128)(2,1)}, bf16[256,128]{1,0:T(8,128)(2,1)S(1)}, u32[]{:S(2)}, u32[]{:S(2)}) collective-permute-start(bf16[256,128]{1,0:T(8,128)(2,1)} %get-tuple-element.280), channel_id=1, source_target_pairs={{0,20},{4,16},{8,28},{12,24},{16,4},{20,0},{24,12},{28,8},{1,21},{... | collective-permute-start | bytes 196616 | tf_op jit(solution)/shard_map/ppermute | solution.py:407
  49.7 6.1 %collective-permute-start.31 = (bf16[256,128]{1,0:T(8,128)(2,1)}, bf16[256,128]{1,0:T(8,128)(2,1)S(1)}, u32[]{:S(2)}, u32[]{:S(2)}) collective-permute-start(bf16[256,128]{1,0:T(8,128)(2,1)} %get-tuple-element.281), channel_id=1, source_target_pairs={{0,24},{4,28},{8,16},{12,20},{16,8},{20,12},{24,0},{28,4},{1,25},{... | collective-permute-start | bytes 196616 | tf_op jit(solution)/shard_map/ppermute | solution.py:407
  53.3 4.8 %collective-permute-start.32 = (bf16[256,128]{1,0:T(8,128)(2,1)}, bf16[256,128]{1,0:T(8,128)(2,1)S(1)}, u32[]{:S(2)}, u32[]{:S(2)}) collective-permute-start(bf16[256,128]{1,0:T(8,128)(2,1)} %get-tuple-element.282), channel_id=1, source_target_pairs={{0,28},{4,24},{8,20},{12,16},{16,12},{20,8},{24,4},{28,0},{1,29},{... | collective-permute-start | bytes 196616 | tf_op jit(solution)/shard_map/ppermute | solution.py:407
  92.7 5.0 %collective-permute-start.42 = (f32[72,128]{1,0:T(8,128)S(1)}, f32[72,128]{1,0:T(8,128)S(1)}, u32[]{:S(2)}, u32[]{:S(2)}) collective-permute-start(f32[72,128]{1,0:T(8,128)S(1)} %add.109), channel_id=1, source_target_pairs={{0,16},{4,20},{8,24},{12,28},{16,0},{20,4},{24,8},{28,12},{1,17},{... | collective-permute-start | bytes 110600 | tf_op jit(solution)/shard_map/ppermute | solution.py:407
  94.3 5.1 %collective-permute-start.43 = (f32[72,128]{1,0:T(8,128)S(1)}, f32[72,128]{1,0:T(8,128)S(1)}, u32[]{:S(2)}, u32[]{:S(2)}) collective-permute-start(f32[72,128]{1,0:T(8,128)S(1)} %add.109), channel_id=1, source_target_pairs={{0,24},{4,28},{8,16},{12,20},{16,8},{20,12},{24,0},{28,4},{1,25},{... | collective-permute-start | bytes 110600 | tf_op jit(solution)/shard_map/ppermute | solution.py:407
  96.2 20.0 %collective-permute-start.33 = (bf16[256,128]{1,0:T(8,128)(2,1)S(1)}, bf16[256,128]{1,0:T(8,128)(2,1)S(1)}, u32[]{:S(2)}, u32[]{:S(2)}) collective-permute-start(bf16[256,128]{1,0:T(8,128)(2,1)S(1)} %get-tuple-element.284), channel_id=1, source_target_pairs={{0,4},{4,0},{8,12},{12,8},{16,20},{20,16},{24,28},{28,24},{1,5},{5... | collective-permute-start | bytes 196616 | tf_op jit(solution)/shard_map/ppermute | solution.py:407
  96.2 20.6 %collective-permute-start.34 = (bf16[256,128]{1,0:T(8,128)(2,1)S(1)}, bf16[256,128]{1,0:T(8,128)(2,1)S(1)}, u32[]{:S(2)}, u32[]{:S(2)}) collective-permute-start(bf16[256,128]{1,0:T(8,128)(2,1)S(1)} %get-tuple-element.285), channel_id=1, source_target_pairs={{0,8},{4,12},{8,0},{12,4},{16,24},{20,28},{24,16},{28,20},{1,9},{5... | collective-permute-start | bytes 196616 | tf_op jit(solution)/shard_map/ppermute | solution.py:407
  100.0 19.1 %collective-permute-start.44 = (f32[72,128]{1,0:T(8,128)S(1)}, f32[72,128]{1,0:T(8,128)S(1)}, u32[]{:S(2)}, u32[]{:S(2)}) collective-permute-start(f32[72,128]{1,0:T(8,128)S(1)} %add_add_fusion.6), channel_id=1, source_target_pairs={{0,1},{1,0},{2,3},{3,2},{4,5},{5,4},{6,7},{7,6},{8,9},{9,8},{10,11... | collective-permute-start | bytes 110600 | tf_op jit(solution)/shard_map/ppermute | solution.py:407
  114.7 6.0 %collective-permute-start.36 = (bf16[256,128]{1,0:T(8,128)(2,1)S(1)}, bf16[256,128]{1,0:T(8,128)(2,1)S(1)}, u32[]{:S(2)}, u32[]{:S(2)}) collective-permute-start(bf16[256,128]{1,0:T(8,128)(2,1)S(1)} %get-tuple-element.287), channel_id=1, source_target_pairs={{0,16},{4,20},{8,24},{12,28},{16,0},{20,4},{24,8},{28,12},{1,17},{... | collective-permute-start | bytes 196616 | tf_op jit(solution)/shard_map/ppermute | solution.py:407
  116.2 6.5 %collective-permute-start.37 = (bf16[256,128]{1,0:T(8,128)(2,1)S(1)}, bf16[256,128]{1,0:T(8,128)(2,1)S(1)}, u32[]{:S(2)}, u32[]{:S(2)}) collective-permute-start(bf16[256,128]{1,0:T(8,128)(2,1)S(1)} %get-tuple-element.288), channel_id=1, source_target_pairs={{0,20},{4,16},{8,28},{12,24},{16,4},{20,0},{24,12},{28,8},{1,21},{... | collective-permute-start | bytes 196616 | tf_op jit(solution)/shard_map/ppermute | solution.py:407
  116.8 5.9 %collective-permute-start.38 = (bf16[256,128]{1,0:T(8,128)(2,1)S(1)}, bf16[256,128]{1,0:T(8,128)(2,1)S(1)}, u32[]{:S(2)}, u32[]{:S(2)}) collective-permute-start(bf16[256,128]{1,0:T(8,128)(2,1)S(1)} %get-tuple-element.289), channel_id=1, source_target_pairs={{0,24},{4,28},{8,16},{12,20},{16,8},{20,12},{24,0},{28,4},{1,25},{... | collective-permute-start | bytes 196616 | tf_op jit(solution)/shard_map/ppermute | solution.py:407
  119.1 7.8 %collective-permute-start.45 = (f32[72,128]{1,0:T(8,128)S(1)}, f32[72,128]{1,0:T(8,128)S(1)}, u32[]{:S(2)}, u32[]{:S(2)}) collective-permute-start(f32[72,128]{1,0:T(8,128)S(1)} %add.113.refs_0_), channel_id=1, source_target_pairs={{0,2},{1,3},{2,0},{3,1},{4,6},{5,7},{6,4},{7,5},{8,10},{9,11},{10,... | collective-permute-start | bytes 110600 | tf_op jit(solution)/shard_map/ppermute | solution.py:407
  126.9 7.3 %collective-permute-start.53 = (f32[72,128]{1,0:T(8,128)S(1)}, f32[72,128]{1,0:T(8,128)S(1)}, u32[]{:S(2)}, u32[]{:S(2)}) collective-permute-start(f32[72,128]{1,0:T(8,128)S(1)} %get-tuple-element.302), channel_id=1, source_target_pairs={{0,4},{4,0},{8,12},{12,8},{16,20},{20,16},{24,28},{28,24},{1,5},{5... | collective-permute-start | bytes 110600 | tf_op jit(solution)/shard_map/ppermute | solution.py:407
  132.9 8.3 %collective-permute-start.46 = (bf16[256,128]{1,0:T(8,128)(2,1)S(1)}, bf16[256,128]{1,0:T(8,128)(2,1)S(1)}, u32[]{:S(2)}, u32[]{:S(2)}) collective-permute-start(bf16[256,128]{1,0:T(8,128)(2,1)S(1)} %get-tuple-element.294), channel_id=1, source_target_pairs={{0,4},{4,0},{8,12},{12,8},{16,20},{20,16},{24,28},{28,24},{1,5},{5... | collective-permute-start | bytes 196616 | tf_op jit(solution)/shard_map/ppermute | solution.py:407
  133.4 9.6 %collective-permute-start.47 = (bf16[256,128]{1,0:T(8,128)(2,1)S(1)}, bf16[256,128]{1,0:T(8,128)(2,1)S(1)}, u32[]{:S(2)}, u32[]{:S(2)}) collective-permute-start(bf16[256,128]{1,0:T(8,128)(2,1)S(1)} %get-tuple-element.295), channel_id=1, source_target_pairs={{0,8},{4,12},{8,0},{12,4},{16,24},{20,28},{24,16},{28,20},{1,9},{5... | collective-permute-start | bytes 196616 | tf_op jit(solution)/shard_map/ppermute | solution.py:407
  135.4 4.9 %collective-permute-start.56 = (f32[72,128]{1,0:T(8,128)S(1)}, f32[72,128]{1,0:T(8,128)S(1)}, u32[]{:S(2)}, u32[]{:S(2)}) collective-permute-start(f32[72,128]{1,0:T(8,128)S(1)} %add.114), channel_id=1, source_target_pairs={{0,24},{4,28},{8,16},{12,20},{16,8},{20,12},{24,0},{28,4},{1,25},{... | collective-permute-start | bytes 110600 | tf_op jit(solution)/shard_map/ppermute | solution.py:407
  138.2 6.4 %collective-permute-start.48 = (bf16[256,128]{1,0:T(8,128)(2,1)S(1)}, bf16[256,128]{1,0:T(8,128)(2,1)S(1)}, u32[]{:S(2)}, u32[]{:S(2)}) collective-permute-start(bf16[256,128]{1,0:T(8,128)(2,1)S(1)} %get-tuple-element.296), channel_id=1, source_target_pairs={{0,12},{4,8},{8,4},{12,0},{16,28},{20,24},{24,20},{28,16},{1,13},{... | collective-permute-start | bytes 196616 | tf_op jit(solution)/shard_map/ppermute | solution.py:407
  141.2 5.8 %collective-permute-start.51 = (bf16[256,128]{1,0:T(8,128)(2,1)S(1)}, bf16[256,128]{1,0:T(8,128)(2,1)S(1)}, u32[]{:S(2)}, u32[]{:S(2)}) collective-permute-start(bf16[256,128]{1,0:T(8,128)(2,1)S(1)} %get-tuple-element.299), channel_id=1, source_target_pairs={{0,24},{4,28},{8,16},{12,20},{16,8},{20,12},{24,0},{28,4},{1,25},{... | collective-permute-start | bytes 196616 | tf_op jit(solution)/shard_map/ppermute | solution.py:407
  143.0 5.0 %collective-permute-start.52 = (bf16[256,128]{1,0:T(8,128)(2,1)S(1)}, bf16[256,128]{1,0:T(8,128)(2,1)S(1)}, u32[]{:S(2)}, u32[]{:S(2)}) collective-permute-start(bf16[256,128]{1,0:T(8,128)(2,1)S(1)} %get-tuple-element.300), channel_id=1, source_target_pairs={{0,28},{4,24},{8,20},{12,16},{16,12},{20,8},{24,4},{28,0},{1,29},{... | collective-permute-start | bytes 196616 | tf_op jit(solution)/shard_map/ppermute | solution.py:407
  144.7 7.6 %collective-permute-start.57 = (f32[72,128]{1,0:T(8,128)S(1)}, f32[72,128]{1,0:T(8,128)S(1)}, u32[]{:S(2)}, u32[]{:S(2)}) collective-permute-start(f32[72,128]{1,0:T(8,128)S(1)} %add_add_fusion.5), channel_id=1, source_target_pairs={{0,1},{1,0},{2,3},{3,2},{4,5},{5,4},{6,7},{7,6},{8,9},{9,8},{10,11... | collective-permute-start | bytes 110600 | tf_op jit(solution)/shard_map/ppermute | solution.py:407
  152.3 5.1 %collective-permute-start.58 = (f32[72,128]{1,0:T(8,128)S(1)}, f32[72,128]{1,0:T(8,128)S(1)}, u32[]{:S(2)}, u32[]{:S(2)}) collective-permute-start(f32[72,128]{1,0:T(8,128)S(1)} %add.118.refs_0_), channel_id=1, source_target_pairs={{0,2},{1,3},{2,0},{3,1},{4,6},{5,7},{6,4},{7,5},{8,10},{9,11},{10,... | collective-permute-start | bytes 110600 | tf_op jit(solution)/shard_map/ppermute | solution.py:407
  153.8 11.1 %collective-permute-start.68 = (f32[72,128]{1,0:T(8,128)S(1)}, f32[72,128]{1,0:T(8,128)S(1)}, u32[]{:S(2)}, u32[]{:S(2)}) collective-permute-start(f32[72,128]{1,0:T(8,128)S(1)} %add.119), channel_id=1, source_target_pairs={{0,16},{4,20},{8,24},{12,28},{16,0},{20,4},{24,8},{28,12},{1,17},{... | collective-permute-start | bytes 110600 | tf_op jit(solution)/shard_map/ppermute | solution.py:407
  154.5 10.4 %collective-permute-start.69 = (f32[72,128]{1,0:T(8,128)S(1)}, f32[72,128]{1,0:T(8,128)S(1)}, u32[]{:S(2)}, u32[]{:S(2)}) collective-permute-start(f32[72,128]{1,0:T(8,128)S(1)} %add.119), channel_id=1, source_target_pairs={{0,24},{4,28},{8,16},{12,20},{16,8},{20,12},{24,0},{28,4},{1,25},{... | collective-permute-start | bytes 110600 | tf_op jit(solution)/shard_map/ppermute | solution.py:407
  156.5 8.5 %collective-permute-start.67 = (f32[72,128]{1,0:T(8,128)S(1)}, f32[72,128]{1,0:T(8,128)S(1)}, u32[]{:S(2)}, u32[]{:S(2)}) collective-permute-start(f32[72,128]{1,0:T(8,128)S(1)} %add.119), channel_id=1, source_target_pairs={{0,8},{4,12},{8,0},{12,4},{16,24},{20,28},{24,16},{28,20},{1,9},{5... | collective-permute-start | bytes 110600 | tf_op jit(solution)/shard_map/ppermute | solution.py:407
  165.0 5.0 %collective-permute-start.70 = (f32[72,128]{1,0:T(8,128)S(1)}, f32[72,128]{1,0:T(8,128)S(1)}, u32[]{:S(2)}, u32[]{:S(2)}) collective-permute-start(f32[72,128]{1,0:T(8,128)S(1)} %add_add_fusion.4), channel_id=1, source_target_pairs={{0,1},{1,0},{2,3},{3,2},{4,5},{5,4},{6,7},{7,6},{8,9},{9,8},{10,11... | collective-permute-start | bytes 110600 | tf_op jit(solution)/shard_map/ppermute | solution.py:407
  165.1 5.0 %collective-permute-start.61 = (bf16[256,128]{1,0:T(8,128)(2,1)S(1)}, bf16[256,128]{1,0:T(8,128)(2,1)S(1)}, u32[]{:S(2)}, u32[]{:S(2)}) collective-permute-start(bf16[256,128]{1,0:T(8,128)(2,1)S(1)} %get-tuple-element.309), channel_id=1, source_target_pairs={{0,12},{4,8},{8,4},{12,0},{16,28},{20,24},{24,20},{28,16},{1,13},{... | collective-permute-start | bytes 196616 | tf_op jit(solution)/shard_map/ppermute | solution.py:407
  165.8 5.9 %collective-permute-start.62 = (bf16[256,128]{1,0:T(8,128)(2,1)S(1)}, bf16[256,128]{1,0:T(8,128)(2,1)S(1)}, u32[]{:S(2)}, u32[]{:S(2)}) collective-permute-start(bf16[256,128]{1,0:T(8,128)(2,1)S(1)} %get-tuple-element.310), channel_id=1, source_target_pairs={{0,16},{4,20},{8,24},{12,28},{16,0},{20,4},{24,8},{28,12},{1,17},{... | collective-permute-start | bytes 196616 | tf_op jit(solution)/shard_map/ppermute | solution.py:407
  166.4 5.3 %collective-permute-start.63 = (bf16[256,128]{1,0:T(8,128)(2,1)S(1)}, bf16[256,128]{1,0:T(8,128)(2,1)S(1)}, u32[]{:S(2)}, u32[]{:S(2)}) collective-permute-start(bf16[256,128]{1,0:T(8,128)(2,1)S(1)} %get-tuple-element.311), channel_id=1, source_target_pairs={{0,20},{4,16},{8,28},{12,24},{16,4},{20,0},{24,12},{28,8},{1,21},{... | collective-permute-start | bytes 196616 | tf_op jit(solution)/shard_map/ppermute | solution.py:407
  168.4 5.2 %collective-permute-start.64 = (bf16[256,128]{1,0:T(8,128)(2,1)S(1)}, bf16[256,128]{1,0:T(8,128)(2,1)S(1)}, u32[]{:S(2)}, u32[]{:S(2)}) collective-permute-start(bf16[256,128]{1,0:T(8,128)(2,1)S(1)} %get-tuple-element.312), channel_id=1, source_target_pairs={{0,24},{4,28},{8,16},{12,20},{16,8},{20,12},{24,0},{28,4},{1,25},{... | collective-permute-start | bytes 196616 | tf_op jit(solution)/shard_map/ppermute | solution.py:407
  170.0 5.0 %collective-permute-start.65 = (bf16[256,128]{1,0:T(8,128)(2,1)S(1)}, bf16[256,128]{1,0:T(8,128)(2,1)S(1)}, u32[]{:S(2)}, u32[]{:S(2)}) collective-permute-start(bf16[256,128]{1,0:T(8,128)(2,1)S(1)} %get-tuple-element.313), channel_id=1, source_target_pairs={{0,28},{4,24},{8,20},{12,16},{16,12},{20,8},{24,4},{28,0},{1,29},{... | collective-permute-start | bytes 196616 | tf_op jit(solution)/shard_map/ppermute | solution.py:407
  170.2 8.0 %collective-permute-start.71 = (f32[72,128]{1,0:T(8,128)S(1)}, f32[72,128]{1,0:T(8,128)S(1)}, u32[]{:S(2)}, u32[]{:S(2)}) collective-permute-start(f32[72,128]{1,0:T(8,128)S(1)} %add.123.refs_0_), channel_id=1, source_target_pairs={{0,2},{1,3},{2,0},{3,1},{4,6},{5,7},{6,4},{7,5},{8,10},{9,11},{10,... | collective-permute-start | bytes 110600 | tf_op jit(solution)/shard_map/ppermute | solution.py:407
  178.1 7.8 %collective-permute-start.79 = (f32[72,128]{1,0:T(8,128)S(1)}, f32[72,128]{1,0:T(8,128)S(1)}, u32[]{:S(2)}, u32[]{:S(2)}) collective-permute-start(f32[72,128]{1,0:T(8,128)S(1)} %get-tuple-element.327), channel_id=1, source_target_pairs={{0,4},{4,0},{8,12},{12,8},{16,20},{20,16},{24,28},{28,24},{1,5},{5... | collective-permute-start | bytes 110600 | tf_op jit(solution)/shard_map/ppermute | solution.py:407
  184.4 8.9 %collective-permute-start.72 = (bf16[256,128]{1,0:T(8,128)(2,1)S(1)}, bf16[256,128]{1,0:T(8,128)(2,1)S(1)}, u32[]{:S(2)}, u32[]{:S(2)}) collective-permute-start(bf16[256,128]{1,0:T(8,128)(2,1)S(1)} %get-tuple-element.319), channel_id=1, source_target_pairs={{0,4},{4,0},{8,12},{12,8},{16,20},{20,16},{24,28},{28,24},{1,5},{5... | collective-permute-start | bytes 196616 | tf_op jit(solution)/shard_map/ppermute | solution.py:407
  184.9 9.8 %collective-permute-start.73 = (bf16[256,128]{1,0:T(8,128)(2,1)S(1)}, bf16[256,128]{1,0:T(8,128)(2,1)S(1)}, u32[]{:S(2)}, u32[]{:S(2)}) collective-permute-start(bf16[256,128]{1,0:T(8,128)(2,1)S(1)} %get-tuple-element.320), channel_id=1, source_target_pairs={{0,8},{4,12},{8,0},{12,4},{16,24},{20,28},{24,16},{28,20},{1,9},{5... | collective-permute-start | bytes 196616 | tf_op jit(solution)/shard_map/ppermute | solution.py:407
  187.1 4.9 %collective-permute-start.82 = (f32[72,128]{1,0:T(8,128)S(1)}, f32[72,128]{1,0:T(8,128)S(1)}, u32[]{:S(2)}, u32[]{:S(2)}) collective-permute-start(f32[72,128]{1,0:T(8,128)S(1)} %add.124), channel_id=1, source_target_pairs={{0,24},{4,28},{8,16},{12,20},{16,8},{20,12},{24,0},{28,4},{1,25},{... | collective-permute-start | bytes 110600 | tf_op jit(solution)/shard_map/ppermute | solution.py:407
  188.5 4.8 %collective-permute-start.80 = (f32[72,128]{1,0:T(8,128)S(1)}, f32[72,128]{1,0:T(8,128)S(1)}, u32[]{:S(2)}, u32[]{:S(2)}) collective-permute-start(f32[72,128]{1,0:T(8,128)S(1)} %add.124), channel_id=1, source_target_pairs={{0,8},{4,12},{8,0},{12,4},{16,24},{20,28},{24,16},{28,20},{1,9},{5... | collective-permute-start | bytes 110600 | tf_op jit(solution)/shard_map/ppermute | solution.py:407
  190.0 6.9 %collective-permute-start.74 = (bf16[256,128]{1,0:T(8,128)(2,1)S(1)}, bf16[256,128]{1,0:T(8,128)(2,1)S(1)}, u32[]{:S(2)}, u32[]{:S(2)}) collective-permute-start(bf16[256,128]{1,0:T(8,128)(2,1)S(1)} %get-tuple-element.321), channel_id=1, source_target_pairs={{0,12},{4,8},{8,4},{12,0},{16,28},{20,24},{24,20},{28,16},{1,13},{... | collective-permute-start | bytes 196616 | tf_op jit(solution)/shard_map/ppermute | solution.py:407
  192.0 6.0 %collective-permute-start.75 = (bf16[256,128]{1,0:T(8,128)(2,1)S(1)}, bf16[256,128]{1,0:T(8,128)(2,1)S(1)}, u32[]{:S(2)}, u32[]{:S(2)}) collective-permute-start(bf16[256,128]{1,0:T(8,128)(2,1)S(1)} %get-tuple-element.322), channel_id=1, source_target_pairs={{0,16},{4,20},{8,24},{12,28},{16,0},{20,4},{24,8},{28,12},{1,17},{... | collective-permute-start | bytes 196616 | tf_op jit(solution)/shard_map/ppermute | solution.py:407
  193.3 5.8 %collective-permute-start.77 = (bf16[256,128]{1,0:T(8,128)(2,1)S(1)}, bf16[256,128]{1,0:T(8,128)(2,1)S(1)}, u32[]{:S(2)}, u32[]{:S(2)}) collective-permute-start(bf16[256,128]{1,0:T(8,128)(2,1)S(1)} %get-tuple-element.324), channel_id=1, source_target_pairs={{0,24},{4,28},{8,16},{12,20},{16,8},{20,12},{24,0},{28,4},{1,25},{... | collective-permute-start | bytes 196616 | tf_op jit(solution)/shard_map/ppermute | solution.py:407
  194.8 5.5 %collective-permute-start.78 = (bf16[256,128]{1,0:T(8,128)(2,1)S(1)}, bf16[256,128]{1,0:T(8,128)(2,1)S(1)}, u32[]{:S(2)}, u32[]{:S(2)}) collective-permute-start(bf16[256,128]{1,0:T(8,128)(2,1)S(1)} %get-tuple-element.325), channel_id=1, source_target_pairs={{0,28},{4,24},{8,20},{12,16},{16,12},{20,8},{24,4},{28,0},{1,29},{... | collective-permute-start | bytes 196616 | tf_op jit(solution)/shard_map/ppermute | solution.py:407
  196.9 7.4 %collective-permute-start.83 = (f32[72,128]{1,0:T(8,128)S(1)}, f32[72,128]{1,0:T(8,128)S(1)}, u32[]{:S(2)}, u32[]{:S(2)}) collective-permute-start(f32[72,128]{1,0:T(8,128)S(1)} %add_add_fusion.3), channel_id=1, source_target_pairs={{0,1},{1,0},{2,3},{3,2},{4,5},{5,4},{6,7},{7,6},{8,9},{9,8},{10,11... | collective-permute-start | bytes 110600 | tf_op jit(solution)/shard_map/ppermute | solution.py:407
  204.3 5.1 %collective-permute-start.84 = (f32[72,128]{1,0:T(8,128)S(1)}, f32[72,128]{1,0:T(8,128)S(1)}, u32[]{:S(2)}, u32[]{:S(2)}) collective-permute-start(f32[72,128]{1,0:T(8,128)S(1)} %add.128.refs_0_), channel_id=1, source_target_pairs={{0,2},{1,3},{2,0},{3,1},{4,6},{5,7},{6,4},{7,5},{8,10},{9,11},{10,... | collective-permute-start | bytes 110600 | tf_op jit(solution)/shard_map/ppermute | solution.py:407
  205.8 10.7 %collective-permute-start.94 = (f32[72,128]{1,0:T(8,128)S(1)}, f32[72,128]{1,0:T(8,128)S(1)}, u32[]{:S(2)}, u32[]{:S(2)}) collective-permute-start(f32[72,128]{1,0:T(8,128)S(1)} %add.130), channel_id=1, source_target_pairs={{0,16},{4,20},{8,24},{12,28},{16,0},{20,4},{24,8},{28,12},{1,17},{... | collective-permute-start | bytes 110600 | tf_op jit(solution)/shard_map/ppermute | solution.py:407
  206.5 10.1 %collective-permute-start.95 = (f32[72,128]{1,0:T(8,128)S(1)}, f32[72,128]{1,0:T(8,128)S(1)}, u32[]{:S(2)}, u32[]{:S(2)}) collective-permute-start(f32[72,128]{1,0:T(8,128)S(1)} %add.130), channel_id=1, source_target_pairs={{0,24},{4,28},{8,16},{12,20},{16,8},{20,12},{24,0},{28,4},{1,25},{... | collective-permute-start | bytes 110600 | tf_op jit(solution)/shard_map/ppermute | solution.py:407
  207.9 8.7 %collective-permute-start.93 = (f32[72,128]{1,0:T(8,128)S(1)}, f32[72,128]{1,0:T(8,128)S(1)}, u32[]{:S(2)}, u32[]{:S(2)}) collective-permute-start(f32[72,128]{1,0:T(8,128)S(1)} %add.130), channel_id=1, source_target_pairs={{0,8},{4,12},{8,0},{12,4},{16,24},{20,28},{24,16},{28,20},{1,9},{5... | collective-permute-start | bytes 110600 | tf_op jit(solution)/shard_map/ppermute | solution.py:407
  215.8 4.7 %collective-permute-start.86 = (bf16[256,128]{1,0:T(8,128)(2,1)S(1)}, bf16[256,128]{1,0:T(8,128)(2,1)S(1)}, u32[]{:S(2)}, u32[]{:S(2)}) collective-permute-start(bf16[256,128]{1,0:T(8,128)(2,1)S(1)} %get-tuple-element.333), channel_id=1, source_target_pairs={{0,8},{4,12},{8,0},{12,4},{16,24},{20,28},{24,16},{28,20},{1,9},{5... | collective-permute-start | bytes 196616 | tf_op jit(solution)/shard_map/ppermute | solution.py:407
  216.6 5.3 %collective-permute-start.96 = (f32[72,128]{1,0:T(8,128)S(1)}, f32[72,128]{1,0:T(8,128)S(1)}, u32[]{:S(2)}, u32[]{:S(2)}) collective-permute-start(f32[72,128]{1,0:T(8,128)S(1)} %add_add_fusion.2), channel_id=1, source_target_pairs={{0,1},{1,0},{2,3},{3,2},{4,5},{5,4},{6,7},{7,6},{8,9},{9,8},{10,11... | collective-permute-start | bytes 110600 | tf_op jit(solution)/shard_map/ppermute | solution.py:407
  218.1 4.8 %collective-permute-start.87 = (bf16[256,128]{1,0:T(8,128)(2,1)S(1)}, bf16[256,128]{1,0:T(8,128)(2,1)S(1)}, u32[]{:S(2)}, u32[]{:S(2)}) collective-permute-start(bf16[256,128]{1,0:T(8,128)(2,1)S(1)} %get-tuple-element.334), channel_id=1, source_target_pairs={{0,12},{4,8},{8,4},{12,0},{16,28},{20,24},{24,20},{28,16},{1,13},{... | collective-permute-start | bytes 196616 | tf_op jit(solution)/shard_map/ppermute | solution.py:407
  218.5 5.9 %collective-permute-start.88 = (bf16[256,128]{1,0:T(8,128)(2,1)S(1)}, bf16[256,128]{1,0:T(8,128)(2,1)S(1)}, u32[]{:S(2)}, u32[]{:S(2)}) collective-permute-start(bf16[256,128]{1,0:T(8,128)(2,1)S(1)} %get-tuple-element.335), channel_id=1, source_target_pairs={{0,16},{4,20},{8,24},{12,28},{16,0},{20,4},{24,8},{28,12},{1,17},{... | collective-permute-start | bytes 196616 | tf_op jit(solution)/shard_map/ppermute | solution.py:407
  219.0 5.4 %collective-permute-start.89 = (bf16[256,128]{1,0:T(8,128)(2,1)S(1)}, bf16[256,128]{1,0:T(8,128)(2,1)S(1)}, u32[]{:S(2)}, u32[]{:S(2)}) collective-permute-start(bf16[256,128]{1,0:T(8,128)(2,1)S(1)} %get-tuple-element.336), channel_id=1, source_target_pairs={{0,20},{4,16},{8,28},{12,24},{16,4},{20,0},{24,12},{28,8},{1,21},{... | collective-permute-start | bytes 196616 | tf_op jit(solution)/shard_map/ppermute | solution.py:407
  220.4 5.2 %collective-permute-start.90 = (bf16[256,128]{1,0:T(8,128)(2,1)S(1)}, bf16[256,128]{1,0:T(8,128)(2,1)S(1)}, u32[]{:S(2)}, u32[]{:S(2)}) collective-permute-start(bf16[256,128]{1,0:T(8,128)(2,1)S(1)} %get-tuple-element.337), channel_id=1, source_target_pairs={{0,24},{4,28},{8,16},{12,20},{16,8},{20,12},{24,0},{28,4},{1,25},{... | collective-permute-start | bytes 196616 | tf_op jit(solution)/shard_map/ppermute | solution.py:407
  221.8 5.2 %collective-permute-start.91 = (bf16[256,128]{1,0:T(8,128)(2,1)S(1)}, bf16[256,128]{1,0:T(8,128)(2,1)S(1)}, u32[]{:S(2)}, u32[]{:S(2)}) collective-permute-start(bf16[256,128]{1,0:T(8,128)(2,1)S(1)} %get-tuple-element.338), channel_id=1, source_target_pairs={{0,28},{4,24},{8,20},{12,16},{16,12},{20,8},{24,4},{28,0},{1,29},{... | collective-permute-start | bytes 196616 | tf_op jit(solution)/shard_map/ppermute | solution.py:407
  222.9 6.9 %collective-permute-start.97 = (f32[72,128]{1,0:T(8,128)S(1)}, f32[72,128]{1,0:T(8,128)S(1)}, u32[]{:S(2)}, u32[]{:S(2)}) collective-permute-start(f32[72,128]{1,0:T(8,128)S(1)} %add.134.refs_0_), channel_id=1, source_target_pairs={{0,2},{1,3},{2,0},{3,1},{4,6},{5,7},{6,4},{7,5},{8,10},{9,11},{10,... | collective-permute-start | bytes 110600 | tf_op jit(solution)/shard_map/ppermute | solution.py:407
  239.1 4.9 %collective-permute-start.101 = (f32[72,128]{1,0:T(8,128)S(1)}, f32[72,128]{1,0:T(8,128)S(1)}, u32[]{:S(2)}, u32[]{:S(2)}) collective-permute-start(f32[72,128]{1,0:T(8,128)S(1)} %add.135), channel_id=1, source_target_pairs={{0,24},{4,28},{8,16},{12,20},{16,8},{20,12},{24,0},{28,4},{1,25},{... | collective-permute-start | bytes 110600 | tf_op jit(solution)/shard_map/ppermute | solution.py:407
  244.3 6.8 %collective-permute-start.102 = (f32[72,128]{1,0:T(8,128)S(1)}, f32[72,128]{1,0:T(8,128)S(1)}, u32[]{:S(2)}, u32[]{:S(2)}) collective-permute-start(f32[72,128]{1,0:T(8,128)S(1)} %add_add_fusion.1.refs_0_), channel_id=1, source_target_pairs={{0,1},{1,0},{2,3},{3,2},{4,5},{5,4},{6,7},{7,6},{8,9},{9,8},{10,11... | collective-permute-start | bytes 110600 | tf_op jit(solution)/shard_map/ppermute | solution.py:407
  245.5 5.6 %collective-permute-start.103 = (f32[72,128]{1,0:T(8,128)S(1)}, f32[72,128]{1,0:T(8,128)S(1)}, u32[]{:S(2)}, u32[]{:S(2)}) collective-permute-start(f32[72,128]{1,0:T(8,128)S(1)} %add_add_fusion.1.refs_0_), channel_id=1, source_target_pairs={{0,2},{1,3},{2,0},{3,1},{4,6},{5,7},{6,4},{7,5},{8,10},{9,11},{10,... | collective-permute-start | bytes 110600 | tf_op jit(solution)/shard_map/ppermute | solution.py:407
  246.8 5.8 %collective-permute-start.104 = (f32[72,128]{1,0:T(8,128)S(1)}, f32[72,128]{1,0:T(8,128)S(1)}, u32[]{:S(2)}, u32[]{:S(2)}) collective-permute-start(f32[72,128]{1,0:T(8,128)S(1)} %add_add_fusion.1.refs_0_), channel_id=1, source_target_pairs={{0,3},{1,2},{2,1},{3,0},{4,7},{5,6},{6,5},{7,4},{8,11},{9,10},{10,... | collective-permute-start | bytes 110600 | tf_op jit(solution)/shard_map/ppermute | solution.py:407
  (34 other events, 268.6 us)
where the time goes:
time: 261 us; the launch traced here: 258 us
  starting transfers between devices  111 us (43%)
  waiting for transfers between devices  78.8 us (30%)
  Pallas kernels  62.3 us (24%)
  local copies, waits for them, and re-layouts  3.91 us (1%)
    ppermute x86, starting transfers between devices, swap(): return lax.ppermute(x, axis, [(i, i ^ d) for i in range(n)])  100 us
    ppermute x86, waiting for transfers between devices, swap(): return lax.ppermute(x, axis, [(i, i ^ d) for i in range(n)])  41.6 us
    ppermute x6, waiting for transfers between devices, shift(): return lax.ppermute(x, axis, [(i, (i + d) % n) for i in range(n)])  37.2 us
    pallas_call x5, Pallas kernels, turn(): pl.pallas_call(functools.partial(turn_kernel, npts, groups, len(parts), f...  31.4 us
    pallas_call x6, Pallas kernels, step(): pl.pallas_call(functools.partial(step_kernel, ncols, groups, first, last)...  18.8 us
    ppermute x6, starting transfers between devices, shift(): return lax.ppermute(x, axis, [(i, (i + d) % n) for i in range(n)])  11.2 us
    pallas_call x1, Pallas kernels, finish(): pl.pallas_call(functools.partial(finish_kernel, npts, len(parts)), out_sh...  5.68 us
  transfers between devices with their start and end apart: 92, of which 35 were waited for; matrix products, arithmetic and copies ran while one was open for 0% of the time, Pallas kernels for 17%

commit v1 on v0

--- a/solution.py
+++ b/solution.py
@@ -21,7 +21,7 @@
 
 
 def params():
-    return pltpu.CompilerParams(vmem_limit_bytes=32 * 1024 * 1024)
+    return pltpu.CompilerParams(vmem_limit_bytes=16 * 1024 * 1024)
 
 
 def find_inverse(send_ref, inverse):

time: 261 us -> 261 us (level)
  no operation moved by 1% of the time
where the time goes in v1:
time: 261 us; the launch traced here: 258 us
  starting transfers between devices  111 us (43%)
  waiting for transfers between devices  78.8 us (30%)
  Pallas kernels  62.3 us (24%)
  local copies, waits for them, and re-layouts  3.91 us (1%)
    ppermute x86, starting transfers between devices, swap(): return lax.ppermute(x, axis, [(i, i ^ d) for i in range(n)])  100 us
    ppermute x86, waiting for transfers between devices, swap(): return lax.ppermute(x, axis, [(i, i ^ d) for i in range(n)])  41.6 us
    ppermute x6, waiting for transfers between devices, shift(): return lax.ppermute(x, axis, [(i, (i + d) % n) for i in range(n)])  37.2 us
    pallas_call x5, Pallas kernels, turn(): pl.pallas_call(functools.partial(turn_kernel, npts, groups, len(parts), f...  31.4 us
    pallas_call x6, Pallas kernels, step(): pl.pallas_call(functools.partial(step_kernel, ncols, groups, first, last)...  18.8 us
    ppermute x6, starting transfers between devices, shift(): return lax.ppermute(x, axis, [(i, (i + d) % n) for i in range(n)])  11.2 us
    pallas_call x1, Pallas kernels, finish(): pl.pallas_call(functools.partial(finish_kernel, npts, len(parts)), out_sh...  5.68 us
  transfers between devices with their start and end apart: 92, of which 35 were waited for; matrix products, arithmetic and copies ran while one was open for 0% of the time, Pallas kernels for 17%

profile of v1, /device:TPU:0, one launch (start us, length us, event | category | flops | bytes accessed | tf_op | source)
XLA Modules:
  0.0 258.5 jit_solution(12702047425829023630)
XLA Ops:
  0.0 2.2 copy-done
  2.9 2.2 shard_map.66
  5.0 3.1 %collective-permute-start.20 = (bf16[800,256]{1,0:T(8,128)(2,1)S(1)}, bf16[800,256]{1,0:T(8,128)(2,1)S(1)}, u32[]{:S(2)}, u32[]{:S(2)}) collective-permute-start(bf16[800,256]{1,0:T(8,128)(2,1)S(1)} %get-tuple-element.265.after_ref), channel_id=1, source_target_pairs={{0,1},{1,2},{2,3},{3,0},{4,5},{5,6},{6,7},{7,4},{8,9},{9,10},{10,1... | collective-permute-start | bytes 1228808 | tf_op jit(solution)/shard_map/ppermute | solution.py:411
  8.1 2.6 %collective-permute-start.21 = (bf16[800,256]{1,0:T(8,128)(2,1)S(1)}, bf16[800,256]{1,0:T(8,128)(2,1)}, u32[]{:S(2)}, u32[]{:S(2)}) collective-permute-start(bf16[800,256]{1,0:T(8,128)(2,1)S(1)} %get-tuple-element.268), channel_id=1, source_target_pairs={{0,2},{1,3},{2,0},{3,1},{4,6},{5,7},{6,4},{7,5},{8,10},{9,11},{10,... | collective-permute-start | bytes 1228808 | tf_op jit(solution)/shard_map/ppermute | solution.py:411
  14.3 1.6 collective-permute-start.14
  17.9 1.5 collective-permute-start.16
  21.4 2.4 collective-permute-start.18
  24.4 1.5 collective-permute-done.18.refs_6_
  28.1 3.1 %collective-permute-start.25 = (bf16[5,256,256]{2,1,0:T(8,128)(2,1)S(1)}, bf16[5,256,256]{2,1,0:T(8,128)(2,1)}, u32[]{:S(2)}, u32[]{:S(2)}) collective-permute-start(bf16[5,256,256]{2,1,0:T(8,128)(2,1)S(1)} %get-tuple-element.274), channel_id=1, source_target_pairs={{0,3},{1,0},{2,1},{3,2},{4,7},{5,4},{6,5},{7,6},{8,11},{9,8},{10,9... | collective-permute-start | bytes 1966088 | tf_op jit(solution)/shard_map/ppermute | solution.py:411
  31.2 7.1 %collective-permute-done.21.refs_10_.refs_2_ = bf16[800,256]{1,0:T(8,128)(2,1)} collective-permute-done((bf16[800,256]{1,0:T(8,128)(2,1)S(1)}, bf16[800,256]{1,0:T(8,128)(2,1)}, u32[]{:S(2)}, u32[]{:S(2)}) %collective-permute-start.21) | collective-permute-done | bytes 409632 | tf_op jit(solution)/shard_map/ppermute | solution.py:411
  38.3 2.2 shard_map.69
  40.5 1.8 collective-permute-start.27
  43.3 2.0 collective-permute-done.27.refs_9_
  45.3 1.8 collective-permute-start.29
  48.3 1.4 collective-permute-done.29.refs_11_
  49.7 3.6 %collective-permute-start.31 = (bf16[256,128]{1,0:T(8,128)(2,1)}, bf16[256,128]{1,0:T(8,128)(2,1)S(1)}, u32[]{:S(2)}, u32[]{:S(2)}) collective-permute-start(bf16[256,128]{1,0:T(8,128)(2,1)} %get-tuple-element.281), channel_id=1, source_target_pairs={{0,24},{4,28},{8,16},{12,20},{16,8},{20,12},{24,0},{28,4},{1,25},{... | collective-permute-start | bytes 196616 | tf_op jit(solution)/shard_map/ppermute | solution.py:407
  54.0 1.9 collective-permute-done.31.refs_13_
  55.8 2.3 collective-permute-done.32.refs_14_
  58.1 30.1 %collective-permute-done.24.refs_5_ = bf16[5,256,256]{2,1,0:T(8,128)(2,1)S(1)} collective-permute-done((bf16[5,256,256]{2,1,0:T(8,128)(2,1)S(1)}, bf16[5,256,256]{2,1,0:T(8,128)(2,1)S(1)}, u32[]{:S(2)}, u32[]{:S(2)}) %collective-permute-start.24) | collective-permute-done | bytes 655392 | tf_op jit(solution)/shard_map/ppermute | solution.py:411
  88.2 3.2 %shard_map.70 = (f32[72,128]{1,0:T(8,128)S(1)}, bf16[256,128]{1,0:T(8,128)(2,1)S(1)}, bf16[256,128]{1,0:T(8,128)(2,1)S(1)}, bf16[256,128]{1,0:T(8,128)(2,1)S(1)}...) custom-call(s32[1,32]{1,0:T(1,128)S(1)} %copy-done.4, ...), custom_call_target="tpu_custom_call" | custom-call | tf_op jit(solution)/shard_map/pallas_call | solution.py:227
  92.7 1.5 collective-permute-start.42
  94.3 1.4 collective-permute-start.43
  96.2 1.5 collective-permute-start.34
  97.7 1.7 collective-permute-done.43
  100.0 14.7 %collective-permute-start.44 = (f32[72,128]{1,0:T(8,128)S(1)}, f32[72,128]{1,0:T(8,128)S(1)}, u32[]{:S(2)}, u32[]{:S(2)}) collective-permute-start(f32[72,128]{1,0:T(8,128)S(1)} %add_add_fusion.6), channel_id=1, source_target_pairs={{0,1},{1,0},{2,3},{3,2},{4,5},{5,4},{6,7},{7,6},{8,9},{9,8},{10,11... | collective-permute-start | bytes 110600 | tf_op jit(solution)/shard_map/ppermute | solution.py:407
  114.7 1.5 collective-permute-start.36
  116.8 2.3 collective-permute-start.38
  119.1 1.5 collective-permute-start.45
  120.7 2.0 collective-permute-done.37.refs_12_
  123.7 3.2 %shard_map.71 = (f32[72,128]{1,0:T(8,128)S(1)}, f32[512,128]{1,0:T(8,128)S(1)}) custom-call(s32[1,32]{1,0:T(1,128)S(1)} %copy-done.4, s32[1,32]{1,0:T(1,128)S(1)} %copy-done.5, s32[1,8]{1,0:T(1,128)S(1)} %get-tuple-element.270.asked_ref, f32[512,128]{1,0:T(8,128)S(1)} %get-tuple-element.271.scale_ref, bf16[8,256,256]{2,1,0:T(8,128)(2,1)S(1)} %get-tuple-element.272.refs_0_, ...), custom_call_target="tpu_custom_call" | custom-call | tf_op jit(solution)/shard_map/pallas_call | solution.py:227
  127.0 5.9 %shard_map.72 = (f32[128,128]{1,0:T(8,128)S(1)}, f32[128,128]{1,0:T(8,128)S(1)}, f32[8,128]{1,0:T(8,128)}, bf16[256,128]{1,0:T(8,128)(2,1)S(1)}, bf16[256,128]{1...) custom-call(s32[1,8]{1,0:T(1,128)S(1)} %get-tuple-element.270.asked_, ...), custom_call_target="tpu_custom_call" | custom-call | tf_op jit(solution)/shard_map/pallas_call | solution.py:294
  135.4 1.5 collective-permute-start.56
  138.2 2.0 collective-permute-done.56
  141.2 1.8 collective-permute-start.51
  143.0 1.7 collective-permute-start.52
  145.6 1.4 collective-permute-done.51.refs_13_
  147.9 3.4 %shard_map.73 = (f32[72,128]{1,0:T(8,128)S(1)}, f32[512,128]{1,0:T(8,128)S(1)}) custom-call(s32[1,32]{1,0:T(1,128)S(1)} %copy-done.4, s32[1,32]{1,0:T(1,128)S(1)} %copy-done.5, s32[1,8]{1,0:T(1,128)S(1)} %get-tuple-element.270.asked_ref, f32[512,128]{1,0:T(8,128)S(1)} %get-tuple-element.271.scale_ref, bf16[8,256,256]{2,1,0:T(8,128)(2,1)S(1)} %get-tuple-element.272.refs_0_, ...), custom_call_target="tpu_custom_call" | custom-call | tf_op jit(solution)/shard_map/pallas_call | solution.py:227
  152.3 1.5 collective-permute-start.58
  154.5 2.0 collective-permute-start.69
  157.4 6.3 %shard_map.74 = (f32[128,128]{1,0:T(8,128)S(1)}, f32[128,128]{1,0:T(8,128)S(1)}, f32[8,128]{1,0:T(8,128)S(1)}, bf16[256,128]{1,0:T(8,128)(2,1)S(1)}, bf16[256,12...) custom-call(s32[1,8]{1,0:T(1,128)S(1)} %get-tuple-element.270.asked_, ...), custom_call_target="tpu_custom_call" | custom-call | tf_op jit(solution)/shard_map/pallas_call | solution.py:294
  168.4 1.6 collective-permute-start.64
  170.2 1.5 collective-permute-start.71
  171.7 1.8 collective-permute-done.64.refs_13_
  173.5 1.4 collective-permute-done.65.refs_14_
  174.9 3.2 %shard_map.75 = (f32[72,128]{1,0:T(8,128)S(1)}, f32[512,128]{1,0:T(8,128)S(1)}) custom-call(s32[1,32]{1,0:T(1,128)S(1)} %copy-done.4, s32[1,32]{1,0:T(1,128)S(1)} %copy-done.5, s32[1,8]{1,0:T(1,128)S(1)} %get-tuple-element.270.asked_ref, f32[512,128]{1,0:T(8,128)S(1)} %get-tuple-element.271.scale_ref, bf16[8,256,256]{2,1,0:T(8,128)(2,1)S(1)} %get-tuple-element.272.refs_0_, ...), custom_call_target="tpu_custom_call" | custom-call | tf_op jit(solution)/shard_map/pallas_call | solution.py:227
  178.2 6.2 %shard_map.76 = (f32[128,128]{1,0:T(8,128)S(1)}, f32[128,128]{1,0:T(8,128)S(1)}, f32[8,128]{1,0:T(8,128)}, bf16[256,128]{1,0:T(8,128)(2,1)S(1)}, bf16[256,128]{1...) custom-call(s32[1,8]{1,0:T(1,128)S(1)} %get-tuple-element.270.asked_, ...), custom_call_target="tpu_custom_call" | custom-call | tf_op jit(solution)/shard_map/pallas_call | solution.py:294
  190.0 2.0 collective-permute-done.82
  193.3 1.4 collective-permute-start.77
  194.8 2.1 collective-permute-start.78
  200.3 3.2 %shard_map.77 = (f32[72,128]{1,0:T(8,128)S(1)}, f32[512,128]{1,0:T(8,128)S(1)}) custom-call(s32[1,32]{1,0:T(1,128)S(1)} %copy-done.4, s32[1,32]{1,0:T(1,128)S(1)} %copy-done.5, s32[1,8]{1,0:T(1,128)S(1)} %get-tuple-element.270.asked_ref, f32[512,128]{1,0:T(8,128)S(1)} %get-tuple-element.271.scale_ref, bf16[8,256,256]{2,1,0:T(8,128)(2,1)S(1)} %get-tuple-element.272.refs_0_, ...), custom_call_target="tpu_custom_call" | custom-call | tf_op jit(solution)/shard_map/pallas_call | solution.py:227
  204.3 1.5 collective-permute-start.84
  207.9 1.5 collective-permute-start.93
  209.4 6.3 %shard_map.78 = (f32[128,128]{1,0:T(8,128)S(1)}, f32[128,128]{1,0:T(8,128)S(1)}, f32[8,128]{1,0:T(8,128)S(1)}, bf16[256,128]{1,0:T(8,128)(2,1)S(1)}, bf16[256,12...) custom-call(s32[1,8]{1,0:T(1,128)S(1)} %get-tuple-element.270.asked_, ...), custom_call_target="tpu_custom_call" | custom-call | tf_op jit(solution)/shard_map/pallas_call | solution.py:294
  216.6 1.5 collective-permute-start.96
  219.0 1.5 collective-permute-start.89
  220.4 1.4 collective-permute-start.90
  222.9 1.5 collective-permute-start.97
  225.7 1.4 collective-permute-done.91.refs_14_
  227.1 2.7 %shard_map.79.p_ref = f32[512,128]{1,0:T(8,128)S(1)} custom-call(s32[1,32]{1,0:T(1,128)S(1)} %copy-done.4, s32[1,32]{1,0:T(1,128)S(1)} %copy-done.5, s32[1,8]{1,0:T(1,128)S(1)} %get-tuple-element.270.asked_ref, f32[512,128]{1,0:T(8,128)S(1)} %get-tuple-element.271.scale_ref, bf16[8,256,256]{2,1,0:T(8,128)(2,1)S(1)} %get-tuple-element.272.refs_0_, ...), custom_call_target="tpu_custom_call" | custom-call | tf_op jit(solution)/shard_map/pallas_call | solution.py:227
  229.8 6.8 %shard_map.80 = (f32[72,128]{1,0:T(8,128)S(1)}, f32[512,128]{1,0:T(8,128)S(1)}) custom-call(s32[1,8]{1,0:T(1,128)S(1)} %get-tuple-element.270.asked_ref, f32[512,128]{1,0:T(8,128)S(1)} %get-tuple-element.271.scale_ref, f32[512,128]{1,0:T(8,128)S(1)} %shard_map.79.p_ref, f32[72,128]{1,0:T(8,128)S(1)} %add.134.refs_0_, ...), custom_call_target="tpu_custom_call" | custom-call | tf_op jit(solution)/shard_map/pallas_call | solution.py:294
  241.9 2.1 collective-permute-done.101
  246.8 1.9 collective-permute-start.104
  251.1 1.5 collective-permute-done.104.refs_3_
  252.6 5.7 %shard_map.81 = bf16[512,128]{1,0:T(8,128)(2,1)} custom-call(f32[512,128]{1,0:T(8,128)S(1)} %get-tuple-element.342.y_ref, f32[72,128]{1,0:T(8,128)S(1)} %add_add_fusion.1.refs_0_, f32[72,128]{1,0:T(8,128)S(1)} %collective-permute-done.102.refs_1_, f32[72,128]{1,0:T(8,128)S(1)} %collective-permute-done.103.refs_2_, f32[72,128]{1,0:T(8,128)S(1)} %collective-permute-done.104.refs_3_), custom_call_target="tpu_custom_call" | custom-call | tf_op jit(solution)/shard_map/pallas_call | solution.py:396
  (168 shorter events, 58.6 us)
Async XLA Ops:
  5.0 23.0 %collective-permute-start.20 = (bf16[800,256]{1,0:T(8,128)(2,1)S(1)}, bf16[800,256]{1,0:T(8,128)(2,1)S(1)}, u32[]{:S(2)}, u32[]{:S(2)}) collective-permute-start(bf16[800,256]{1,0:T(8,128)(2,1)S(1)} %get-tuple-element.265.after_ref), channel_id=1, source_target_pairs={{0,1},{1,2},{2,3},{3,0},{4,5},{5,6},{6,7},{7,4},{8,9},{9,10},{10,1... | collective-permute-start | bytes 1228808 | tf_op jit(solution)/shard_map/ppermute | solution.py:411
  8.1 30.2 %collective-permute-start.21 = (bf16[800,256]{1,0:T(8,128)(2,1)S(1)}, bf16[800,256]{1,0:T(8,128)(2,1)}, u32[]{:S(2)}, u32[]{:S(2)}) collective-permute-start(bf16[800,256]{1,0:T(8,128)(2,1)S(1)} %get-tuple-element.268), channel_id=1, source_target_pairs={{0,2},{1,3},{2,0},{3,1},{4,6},{5,7},{6,4},{7,5},{8,10},{9,11},{10,... | collective-permute-start | bytes 1228808 | tf_op jit(solution)/shard_map/ppermute | solution.py:411
  10.7 27.6 %collective-permute-start.22 = (bf16[800,256]{1,0:T(8,128)(2,1)S(1)}, bf16[800,256]{1,0:T(8,128)(2,1)}, u32[]{:S(2)}, u32[]{:S(2)}) collective-permute-start(bf16[800,256]{1,0:T(8,128)(2,1)S(1)} %get-tuple-element.269), channel_id=1, source_target_pairs={{0,3},{1,0},{2,1},{3,2},{4,7},{5,4},{6,5},{7,6},{8,11},{9,8},{10,9... | collective-permute-start | bytes 1228808 | tf_op jit(solution)/shard_map/ppermute | solution.py:411
  25.9 32.3 %collective-permute-start.23 = (bf16[5,256,256]{2,1,0:T(8,128)(2,1)S(1)}, bf16[5,256,256]{2,1,0:T(8,128)(2,1)S(1)}, u32[]{:S(2)}, u32[]{:S(2)}) collective-permute-start(bf16[5,256,256]{2,1,0:T(8,128)(2,1)S(1)} %get-tuple-element.266.after_ref), channel_id=1, source_target_pairs={{0,1},{1,2},{2,3},{3,0},{4,5},{5,6},{6,7},{7,4},{8,9},{9,10},{10,1... | collective-permute-start | bytes 1966088 | tf_op jit(solution)/shard_map/ppermute | solution.py:411
  27.7 60.5 %collective-permute-start.24 = (bf16[5,256,256]{2,1,0:T(8,128)(2,1)S(1)}, bf16[5,256,256]{2,1,0:T(8,128)(2,1)S(1)}, u32[]{:S(2)}, u32[]{:S(2)}) collective-permute-start(bf16[5,256,256]{2,1,0:T(8,128)(2,1)S(1)} %get-tuple-element.273), channel_id=1, source_target_pairs={{0,2},{1,3},{2,0},{3,1},{4,6},{5,7},{6,4},{7,5},{8,10},{9,11},{10,... | collective-permute-start | bytes 1966088 | tf_op jit(solution)/shard_map/ppermute | solution.py:411
  28.1 60.2 %collective-permute-start.25 = (bf16[5,256,256]{2,1,0:T(8,128)(2,1)S(1)}, bf16[5,256,256]{2,1,0:T(8,128)(2,1)}, u32[]{:S(2)}, u32[]{:S(2)}) collective-permute-start(bf16[5,256,256]{2,1,0:T(8,128)(2,1)S(1)} %get-tuple-element.274), channel_id=1, source_target_pairs={{0,3},{1,0},{2,1},{3,2},{4,7},{5,4},{6,5},{7,6},{8,11},{9,8},{10,9... | collective-permute-start | bytes 1966088 | tf_op jit(solution)/shard_map/ppermute | solution.py:411
  40.5 4.7 %collective-permute-start.27 = (bf16[256,128]{1,0:T(8,128)(2,1)}, bf16[256,128]{1,0:T(8,128)(2,1)S(1)}, u32[]{:S(2)}, u32[]{:S(2)}) collective-permute-start(bf16[256,128]{1,0:T(8,128)(2,1)} %get-tuple-element.277), channel_id=1, source_target_pairs={{0,8},{4,12},{8,0},{12,4},{16,24},{20,28},{24,16},{28,20},{1,9},{5... | collective-permute-start | bytes 196616 | tf_op jit(solution)/shard_map/ppermute | solution.py:407
  47.0 6.3 %collective-permute-start.30 = (bf16[256,128]{1,0:T(8,128)(2,1)}, bf16[256,128]{1,0:T(8,128)(2,1)S(1)}, u32[]{:S(2)}, u32[]{:S(2)}) collective-permute-start(bf16[256,128]{1,0:T(8,128)(2,1)} %get-tuple-element.280), channel_id=1, source_target_pairs={{0,20},{4,16},{8,28},{12,24},{16,4},{20,0},{24,12},{28,8},{1,21},{... | collective-permute-start | bytes 196616 | tf_op jit(solution)/shard_map/ppermute | solution.py:407
  49.7 6.1 %collective-permute-start.31 = (bf16[256,128]{1,0:T(8,128)(2,1)}, bf16[256,128]{1,0:T(8,128)(2,1)S(1)}, u32[]{:S(2)}, u32[]{:S(2)}) collective-permute-start(bf16[256,128]{1,0:T(8,128)(2,1)} %get-tuple-element.281), channel_id=1, source_target_pairs={{0,24},{4,28},{8,16},{12,20},{16,8},{20,12},{24,0},{28,4},{1,25},{... | collective-permute-start | bytes 196616 | tf_op jit(solution)/shard_map/ppermute | solution.py:407
  53.3 4.8 %collective-permute-start.32 = (bf16[256,128]{1,0:T(8,128)(2,1)}, bf16[256,128]{1,0:T(8,128)(2,1)S(1)}, u32[]{:S(2)}, u32[]{:S(2)}) collective-permute-start(bf16[256,128]{1,0:T(8,128)(2,1)} %get-tuple-element.282), channel_id=1, source_target_pairs={{0,28},{4,24},{8,20},{12,16},{16,12},{20,8},{24,4},{28,0},{1,29},{... | collective-permute-start | bytes 196616 | tf_op jit(solution)/shard_map/ppermute | solution.py:407
  92.7 5.0 %collective-permute-start.42 = (f32[72,128]{1,0:T(8,128)S(1)}, f32[72,128]{1,0:T(8,128)S(1)}, u32[]{:S(2)}, u32[]{:S(2)}) collective-permute-start(f32[72,128]{1,0:T(8,128)S(1)} %add.109), channel_id=1, source_target_pairs={{0,16},{4,20},{8,24},{12,28},{16,0},{20,4},{24,8},{28,12},{1,17},{... | collective-permute-start | bytes 110600 | tf_op jit(solution)/shard_map/ppermute | solution.py:407
  94.3 5.1 %collective-permute-start.43 = (f32[72,128]{1,0:T(8,128)S(1)}, f32[72,128]{1,0:T(8,128)S(1)}, u32[]{:S(2)}, u32[]{:S(2)}) collective-permute-start(f32[72,128]{1,0:T(8,128)S(1)} %add.109), channel_id=1, source_target_pairs={{0,24},{4,28},{8,16},{12,20},{16,8},{20,12},{24,0},{28,4},{1,25},{... | collective-permute-start | bytes 110600 | tf_op jit(solution)/shard_map/ppermute | solution.py:407
  96.2 20.0 %collective-permute-start.33 = (bf16[256,128]{1,0:T(8,128)(2,1)S(1)}, bf16[256,128]{1,0:T(8,128)(2,1)S(1)}, u32[]{:S(2)}, u32[]{:S(2)}) collective-permute-start(bf16[256,128]{1,0:T(8,128)(2,1)S(1)} %get-tuple-element.284), channel_id=1, source_target_pairs={{0,4},{4,0},{8,12},{12,8},{16,20},{20,16},{24,28},{28,24},{1,5},{5... | collective-permute-start | bytes 196616 | tf_op jit(solution)/shard_map/ppermute | solution.py:407
  96.2 20.6 %collective-permute-start.34 = (bf16[256,128]{1,0:T(8,128)(2,1)S(1)}, bf16[256,128]{1,0:T(8,128)(2,1)S(1)}, u32[]{:S(2)}, u32[]{:S(2)}) collective-permute-start(bf16[256,128]{1,0:T(8,128)(2,1)S(1)} %get-tuple-element.285), channel_id=1, source_target_pairs={{0,8},{4,12},{8,0},{12,4},{16,24},{20,28},{24,16},{28,20},{1,9},{5... | collective-permute-start | bytes 196616 | tf_op jit(solution)/shard_map/ppermute | solution.py:407
  100.0 19.1 %collective-permute-start.44 = (f32[72,128]{1,0:T(8,128)S(1)}, f32[72,128]{1,0:T(8,128)S(1)}, u32[]{:S(2)}, u32[]{:S(2)}) collective-permute-start(f32[72,128]{1,0:T(8,128)S(1)} %add_add_fusion.6), channel_id=1, source_target_pairs={{0,1},{1,0},{2,3},{3,2},{4,5},{5,4},{6,7},{7,6},{8,9},{9,8},{10,11... | collective-permute-start | bytes 110600 | tf_op jit(solution)/shard_map/ppermute | solution.py:407
  114.7 6.0 %collective-permute-start.36 = (bf16[256,128]{1,0:T(8,128)(2,1)S(1)}, bf16[256,128]{1,0:T(8,128)(2,1)S(1)}, u32[]{:S(2)}, u32[]{:S(2)}) collective-permute-start(bf16[256,128]{1,0:T(8,128)(2,1)S(1)} %get-tuple-element.287), channel_id=1, source_target_pairs={{0,16},{4,20},{8,24},{12,28},{16,0},{20,4},{24,8},{28,12},{1,17},{... | collective-permute-start | bytes 196616 | tf_op jit(solution)/shard_map/ppermute | solution.py:407
  116.2 6.5 %collective-permute-start.37 = (bf16[256,128]{1,0:T(8,128)(2,1)S(1)}, bf16[256,128]{1,0:T(8,128)(2,1)S(1)}, u32[]{:S(2)}, u32[]{:S(2)}) collective-permute-start(bf16[256,128]{1,0:T(8,128)(2,1)S(1)} %get-tuple-element.288), channel_id=1, source_target_pairs={{0,20},{4,16},{8,28},{12,24},{16,4},{20,0},{24,12},{28,8},{1,21},{... | collective-permute-start | bytes 196616 | tf_op jit(solution)/shard_map/ppermute | solution.py:407
  116.8 5.9 %collective-permute-start.38 = (bf16[256,128]{1,0:T(8,128)(2,1)S(1)}, bf16[256,128]{1,0:T(8,128)(2,1)S(1)}, u32[]{:S(2)}, u32[]{:S(2)}) collective-permute-start(bf16[256,128]{1,0:T(8,128)(2,1)S(1)} %get-tuple-element.289), channel_id=1, source_target_pairs={{0,24},{4,28},{8,16},{12,20},{16,8},{20,12},{24,0},{28,4},{1,25},{... | collective-permute-start | bytes 196616 | tf_op jit(solution)/shard_map/ppermute | solution.py:407
  119.1 7.8 %collective-permute-start.45 = (f32[72,128]{1,0:T(8,128)S(1)}, f32[72,128]{1,0:T(8,128)S(1)}, u32[]{:S(2)}, u32[]{:S(2)}) collective-permute-start(f32[72,128]{1,0:T(8,128)S(1)} %add.113.refs_0_), channel_id=1, source_target_pairs={{0,2},{1,3},{2,0},{3,1},{4,6},{5,7},{6,4},{7,5},{8,10},{9,11},{10,... | collective-permute-start | bytes 110600 | tf_op jit(solution)/shard_map/ppermute | solution.py:407
  126.9 7.3 %collective-permute-start.53 = (f32[72,128]{1,0:T(8,128)S(1)}, f32[72,128]{1,0:T(8,128)S(1)}, u32[]{:S(2)}, u32[]{:S(2)}) collective-permute-start(f32[72,128]{1,0:T(8,128)S(1)} %get-tuple-element.302), channel_id=1, source_target_pairs={{0,4},{4,0},{8,12},{12,8},{16,20},{20,16},{24,28},{28,24},{1,5},{5... | collective-permute-start | bytes 110600 | tf_op jit(solution)/shard_map/ppermute | solution.py:407
  132.9 8.3 %collective-permute-start.46 = (bf16[256,128]{1,0:T(8,128)(2,1)S(1)}, bf16[256,128]{1,0:T(8,128)(2,1)S(1)}, u32[]{:S(2)}, u32[]{:S(2)}) collective-permute-start(bf16[256,128]{1,0:T(8,128)(2,1)S(1)} %get-tuple-element.294), channel_id=1, source_target_pairs={{0,4},{4,0},{8,12},{12,8},{16,20},{20,16},{24,28},{28,24},{1,5},{5... | collective-permute-start | bytes 196616 | tf_op jit(solution)/shard_map/ppermute | solution.py:407
  133.4 9.6 %collective-permute-start.47 = (bf16[256,128]{1,0:T(8,128)(2,1)S(1)}, bf16[256,128]{1,0:T(8,128)(2,1)S(1)}, u32[]{:S(2)}, u32[]{:S(2)}) collective-permute-start(bf16[256,128]{1,0:T(8,128)(2,1)S(1)} %get-tuple-element.295), channel_id=1, source_target_pairs={{0,8},{4,12},{8,0},{12,4},{16,24},{20,28},{24,16},{28,20},{1,9},{5... | collective-permute-start | bytes 196616 | tf_op jit(solution)/shard_map/ppermute | solution.py:407
  135.4 4.9 %collective-permute-start.56 = (f32[72,128]{1,0:T(8,128)S(1)}, f32[72,128]{1,0:T(8,128)S(1)}, u32[]{:S(2)}, u32[]{:S(2)}) collective-permute-start(f32[72,128]{1,0:T(8,128)S(1)} %add.114), channel_id=1, source_target_pairs={{0,24},{4,28},{8,16},{12,20},{16,8},{20,12},{24,0},{28,4},{1,25},{... | collective-permute-start | bytes 110600 | tf_op jit(solution)/shard_map/ppermute | solution.py:407
  138.2 6.5 %collective-permute-start.48 = (bf16[256,128]{1,0:T(8,128)(2,1)S(1)}, bf16[256,128]{1,0:T(8,128)(2,1)S(1)}, u32[]{:S(2)}, u32[]{:S(2)}) collective-permute-start(bf16[256,128]{1,0:T(8,128)(2,1)S(1)} %get-tuple-element.296), channel_id=1, source_target_pairs={{0,12},{4,8},{8,4},{12,0},{16,28},{20,24},{24,20},{28,16},{1,13},{... | collective-permute-start | bytes 196616 | tf_op jit(solution)/shard_map/ppermute | solution.py:407
  141.2 5.8 %collective-permute-start.51 = (bf16[256,128]{1,0:T(8,128)(2,1)S(1)}, bf16[256,128]{1,0:T(8,128)(2,1)S(1)}, u32[]{:S(2)}, u32[]{:S(2)}) collective-permute-start(bf16[256,128]{1,0:T(8,128)(2,1)S(1)} %get-tuple-element.299), channel_id=1, source_target_pairs={{0,24},{4,28},{8,16},{12,20},{16,8},{20,12},{24,0},{28,4},{1,25},{... | collective-permute-start | bytes 196616 | tf_op jit(solution)/shard_map/ppermute | solution.py:407
  143.0 5.0 %collective-permute-start.52 = (bf16[256,128]{1,0:T(8,128)(2,1)S(1)}, bf16[256,128]{1,0:T(8,128)(2,1)S(1)}, u32[]{:S(2)}, u32[]{:S(2)}) collective-permute-start(bf16[256,128]{1,0:T(8,128)(2,1)S(1)} %get-tuple-element.300), channel_id=1, source_target_pairs={{0,28},{4,24},{8,20},{12,16},{16,12},{20,8},{24,4},{28,0},{1,29},{... | collective-permute-start | bytes 196616 | tf_op jit(solution)/shard_map/ppermute | solution.py:407
  144.7 7.6 %collective-permute-start.57 = (f32[72,128]{1,0:T(8,128)S(1)}, f32[72,128]{1,0:T(8,128)S(1)}, u32[]{:S(2)}, u32[]{:S(2)}) collective-permute-start(f32[72,128]{1,0:T(8,128)S(1)} %add_add_fusion.5), channel_id=1, source_target_pairs={{0,1},{1,0},{2,3},{3,2},{4,5},{5,4},{6,7},{7,6},{8,9},{9,8},{10,11... | collective-permute-start | bytes 110600 | tf_op jit(solution)/shard_map/ppermute | solution.py:407
  152.3 5.1 %collective-permute-start.58 = (f32[72,128]{1,0:T(8,128)S(1)}, f32[72,128]{1,0:T(8,128)S(1)}, u32[]{:S(2)}, u32[]{:S(2)}) collective-permute-start(f32[72,128]{1,0:T(8,128)S(1)} %add.118.refs_0_), channel_id=1, source_target_pairs={{0,2},{1,3},{2,0},{3,1},{4,6},{5,7},{6,4},{7,5},{8,10},{9,11},{10,... | collective-permute-start | bytes 110600 | tf_op jit(solution)/shard_map/ppermute | solution.py:407
  153.8 11.1 %collective-permute-start.68 = (f32[72,128]{1,0:T(8,128)S(1)}, f32[72,128]{1,0:T(8,128)S(1)}, u32[]{:S(2)}, u32[]{:S(2)}) collective-permute-start(f32[72,128]{1,0:T(8,128)S(1)} %add.119), channel_id=1, source_target_pairs={{0,16},{4,20},{8,24},{12,28},{16,0},{20,4},{24,8},{28,12},{1,17},{... | collective-permute-start | bytes 110600 | tf_op jit(solution)/shard_map/ppermute | solution.py:407
  154.5 10.4 %collective-permute-start.69 = (f32[72,128]{1,0:T(8,128)S(1)}, f32[72,128]{1,0:T(8,128)S(1)}, u32[]{:S(2)}, u32[]{:S(2)}) collective-permute-start(f32[72,128]{1,0:T(8,128)S(1)} %add.119), channel_id=1, source_target_pairs={{0,24},{4,28},{8,16},{12,20},{16,8},{20,12},{24,0},{28,4},{1,25},{... | collective-permute-start | bytes 110600 | tf_op jit(solution)/shard_map/ppermute | solution.py:407
  156.5 8.5 %collective-permute-start.67 = (f32[72,128]{1,0:T(8,128)S(1)}, f32[72,128]{1,0:T(8,128)S(1)}, u32[]{:S(2)}, u32[]{:S(2)}) collective-permute-start(f32[72,128]{1,0:T(8,128)S(1)} %add.119), channel_id=1, source_target_pairs={{0,8},{4,12},{8,0},{12,4},{16,24},{20,28},{24,16},{28,20},{1,9},{5... | collective-permute-start | bytes 110600 | tf_op jit(solution)/shard_map/ppermute | solution.py:407
  165.0 5.0 %collective-permute-start.70 = (f32[72,128]{1,0:T(8,128)S(1)}, f32[72,128]{1,0:T(8,128)S(1)}, u32[]{:S(2)}, u32[]{:S(2)}) collective-permute-start(f32[72,128]{1,0:T(8,128)S(1)} %add_add_fusion.4), channel_id=1, source_target_pairs={{0,1},{1,0},{2,3},{3,2},{4,5},{5,4},{6,7},{7,6},{8,9},{9,8},{10,11... | collective-permute-start | bytes 110600 | tf_op jit(solution)/shard_map/ppermute | solution.py:407
  165.1 5.0 %collective-permute-start.61 = (bf16[256,128]{1,0:T(8,128)(2,1)S(1)}, bf16[256,128]{1,0:T(8,128)(2,1)S(1)}, u32[]{:S(2)}, u32[]{:S(2)}) collective-permute-start(bf16[256,128]{1,0:T(8,128)(2,1)S(1)} %get-tuple-element.309), channel_id=1, source_target_pairs={{0,12},{4,8},{8,4},{12,0},{16,28},{20,24},{24,20},{28,16},{1,13},{... | collective-permute-start | bytes 196616 | tf_op jit(solution)/shard_map/ppermute | solution.py:407
  165.8 6.0 %collective-permute-start.62 = (bf16[256,128]{1,0:T(8,128)(2,1)S(1)}, bf16[256,128]{1,0:T(8,128)(2,1)S(1)}, u32[]{:S(2)}, u32[]{:S(2)}) collective-permute-start(bf16[256,128]{1,0:T(8,128)(2,1)S(1)} %get-tuple-element.310), channel_id=1, source_target_pairs={{0,16},{4,20},{8,24},{12,28},{16,0},{20,4},{24,8},{28,12},{1,17},{... | collective-permute-start | bytes 196616 | tf_op jit(solution)/shard_map/ppermute | solution.py:407
  166.4 5.3 %collective-permute-start.63 = (bf16[256,128]{1,0:T(8,128)(2,1)S(1)}, bf16[256,128]{1,0:T(8,128)(2,1)S(1)}, u32[]{:S(2)}, u32[]{:S(2)}) collective-permute-start(bf16[256,128]{1,0:T(8,128)(2,1)S(1)} %get-tuple-element.311), channel_id=1, source_target_pairs={{0,20},{4,16},{8,28},{12,24},{16,4},{20,0},{24,12},{28,8},{1,21},{... | collective-permute-start | bytes 196616 | tf_op jit(solution)/shard_map/ppermute | solution.py:407
  168.4 5.2 %collective-permute-start.64 = (bf16[256,128]{1,0:T(8,128)(2,1)S(1)}, bf16[256,128]{1,0:T(8,128)(2,1)S(1)}, u32[]{:S(2)}, u32[]{:S(2)}) collective-permute-start(bf16[256,128]{1,0:T(8,128)(2,1)S(1)} %get-tuple-element.312), channel_id=1, source_target_pairs={{0,24},{4,28},{8,16},{12,20},{16,8},{20,12},{24,0},{28,4},{1,25},{... | collective-permute-start | bytes 196616 | tf_op jit(solution)/shard_map/ppermute | solution.py:407
  170.0 5.0 %collective-permute-start.65 = (bf16[256,128]{1,0:T(8,128)(2,1)S(1)}, bf16[256,128]{1,0:T(8,128)(2,1)S(1)}, u32[]{:S(2)}, u32[]{:S(2)}) collective-permute-start(bf16[256,128]{1,0:T(8,128)(2,1)S(1)} %get-tuple-element.313), channel_id=1, source_target_pairs={{0,28},{4,24},{8,20},{12,16},{16,12},{20,8},{24,4},{28,0},{1,29},{... | collective-permute-start | bytes 196616 | tf_op jit(solution)/shard_map/ppermute | solution.py:407
  170.2 8.0 %collective-permute-start.71 = (f32[72,128]{1,0:T(8,128)S(1)}, f32[72,128]{1,0:T(8,128)S(1)}, u32[]{:S(2)}, u32[]{:S(2)}) collective-permute-start(f32[72,128]{1,0:T(8,128)S(1)} %add.123.refs_0_), channel_id=1, source_target_pairs={{0,2},{1,3},{2,0},{3,1},{4,6},{5,7},{6,4},{7,5},{8,10},{9,11},{10,... | collective-permute-start | bytes 110600 | tf_op jit(solution)/shard_map/ppermute | solution.py:407
  178.1 7.8 %collective-permute-start.79 = (f32[72,128]{1,0:T(8,128)S(1)}, f32[72,128]{1,0:T(8,128)S(1)}, u32[]{:S(2)}, u32[]{:S(2)}) collective-permute-start(f32[72,128]{1,0:T(8,128)S(1)} %get-tuple-element.327), channel_id=1, source_target_pairs={{0,4},{4,0},{8,12},{12,8},{16,20},{20,16},{24,28},{28,24},{1,5},{5... | collective-permute-start | bytes 110600 | tf_op jit(solution)/shard_map/ppermute | solution.py:407
  184.4 8.9 %collective-permute-start.72 = (bf16[256,128]{1,0:T(8,128)(2,1)S(1)}, bf16[256,128]{1,0:T(8,128)(2,1)S(1)}, u32[]{:S(2)}, u32[]{:S(2)}) collective-permute-start(bf16[256,128]{1,0:T(8,128)(2,1)S(1)} %get-tuple-element.319), channel_id=1, source_target_pairs={{0,4},{4,0},{8,12},{12,8},{16,20},{20,16},{24,28},{28,24},{1,5},{5... | collective-permute-start | bytes 196616 | tf_op jit(solution)/shard_map/ppermute | solution.py:407
  184.9 9.9 %collective-permute-start.73 = (bf16[256,128]{1,0:T(8,128)(2,1)S(1)}, bf16[256,128]{1,0:T(8,128)(2,1)S(1)}, u32[]{:S(2)}, u32[]{:S(2)}) collective-permute-start(bf16[256,128]{1,0:T(8,128)(2,1)S(1)} %get-tuple-element.320), channel_id=1, source_target_pairs={{0,8},{4,12},{8,0},{12,4},{16,24},{20,28},{24,16},{28,20},{1,9},{5... | collective-permute-start | bytes 196616 | tf_op jit(solution)/shard_map/ppermute | solution.py:407
  187.2 4.9 %collective-permute-start.82 = (f32[72,128]{1,0:T(8,128)S(1)}, f32[72,128]{1,0:T(8,128)S(1)}, u32[]{:S(2)}, u32[]{:S(2)}) collective-permute-start(f32[72,128]{1,0:T(8,128)S(1)} %add.124), channel_id=1, source_target_pairs={{0,24},{4,28},{8,16},{12,20},{16,8},{20,12},{24,0},{28,4},{1,25},{... | collective-permute-start | bytes 110600 | tf_op jit(solution)/shard_map/ppermute | solution.py:407
  188.5 4.8 %collective-permute-start.80 = (f32[72,128]{1,0:T(8,128)S(1)}, f32[72,128]{1,0:T(8,128)S(1)}, u32[]{:S(2)}, u32[]{:S(2)}) collective-permute-start(f32[72,128]{1,0:T(8,128)S(1)} %add.124), channel_id=1, source_target_pairs={{0,8},{4,12},{8,0},{12,4},{16,24},{20,28},{24,16},{28,20},{1,9},{5... | collective-permute-start | bytes 110600 | tf_op jit(solution)/shard_map/ppermute | solution.py:407
  190.0 6.9 %collective-permute-start.74 = (bf16[256,128]{1,0:T(8,128)(2,1)S(1)}, bf16[256,128]{1,0:T(8,128)(2,1)S(1)}, u32[]{:S(2)}, u32[]{:S(2)}) collective-permute-start(bf16[256,128]{1,0:T(8,128)(2,1)S(1)} %get-tuple-element.321), channel_id=1, source_target_pairs={{0,12},{4,8},{8,4},{12,0},{16,28},{20,24},{24,20},{28,16},{1,13},{... | collective-permute-start | bytes 196616 | tf_op jit(solution)/shard_map/ppermute | solution.py:407
  192.0 5.9 %collective-permute-start.75 = (bf16[256,128]{1,0:T(8,128)(2,1)S(1)}, bf16[256,128]{1,0:T(8,128)(2,1)S(1)}, u32[]{:S(2)}, u32[]{:S(2)}) collective-permute-start(bf16[256,128]{1,0:T(8,128)(2,1)S(1)} %get-tuple-element.322), channel_id=1, source_target_pairs={{0,16},{4,20},{8,24},{12,28},{16,0},{20,4},{24,8},{28,12},{1,17},{... | collective-permute-start | bytes 196616 | tf_op jit(solution)/shard_map/ppermute | solution.py:407
  193.3 5.8 %collective-permute-start.77 = (bf16[256,128]{1,0:T(8,128)(2,1)S(1)}, bf16[256,128]{1,0:T(8,128)(2,1)S(1)}, u32[]{:S(2)}, u32[]{:S(2)}) collective-permute-start(bf16[256,128]{1,0:T(8,128)(2,1)S(1)} %get-tuple-element.324), channel_id=1, source_target_pairs={{0,24},{4,28},{8,16},{12,20},{16,8},{20,12},{24,0},{28,4},{1,25},{... | collective-permute-start | bytes 196616 | tf_op jit(solution)/shard_map/ppermute | solution.py:407
  194.8 5.5 %collective-permute-start.78 = (bf16[256,128]{1,0:T(8,128)(2,1)S(1)}, bf16[256,128]{1,0:T(8,128)(2,1)S(1)}, u32[]{:S(2)}, u32[]{:S(2)}) collective-permute-start(bf16[256,128]{1,0:T(8,128)(2,1)S(1)} %get-tuple-element.325), channel_id=1, source_target_pairs={{0,28},{4,24},{8,20},{12,16},{16,12},{20,8},{24,4},{28,0},{1,29},{... | collective-permute-start | bytes 196616 | tf_op jit(solution)/shard_map/ppermute | solution.py:407
  196.9 7.4 %collective-permute-start.83 = (f32[72,128]{1,0:T(8,128)S(1)}, f32[72,128]{1,0:T(8,128)S(1)}, u32[]{:S(2)}, u32[]{:S(2)}) collective-permute-start(f32[72,128]{1,0:T(8,128)S(1)} %add_add_fusion.3), channel_id=1, source_target_pairs={{0,1},{1,0},{2,3},{3,2},{4,5},{5,4},{6,7},{7,6},{8,9},{9,8},{10,11... | collective-permute-start | bytes 110600 | tf_op jit(solution)/shard_map/ppermute | solution.py:407
  204.3 5.1 %collective-permute-start.84 = (f32[72,128]{1,0:T(8,128)S(1)}, f32[72,128]{1,0:T(8,128)S(1)}, u32[]{:S(2)}, u32[]{:S(2)}) collective-permute-start(f32[72,128]{1,0:T(8,128)S(1)} %add.128.refs_0_), channel_id=1, source_target_pairs={{0,2},{1,3},{2,0},{3,1},{4,6},{5,7},{6,4},{7,5},{8,10},{9,11},{10,... | collective-permute-start | bytes 110600 | tf_op jit(solution)/shard_map/ppermute | solution.py:407
  205.8 10.7 %collective-permute-start.94 = (f32[72,128]{1,0:T(8,128)S(1)}, f32[72,128]{1,0:T(8,128)S(1)}, u32[]{:S(2)}, u32[]{:S(2)}) collective-permute-start(f32[72,128]{1,0:T(8,128)S(1)} %add.130), channel_id=1, source_target_pairs={{0,16},{4,20},{8,24},{12,28},{16,0},{20,4},{24,8},{28,12},{1,17},{... | collective-permute-start | bytes 110600 | tf_op jit(solution)/shard_map/ppermute | solution.py:407
  206.5 10.1 %collective-permute-start.95 = (f32[72,128]{1,0:T(8,128)S(1)}, f32[72,128]{1,0:T(8,128)S(1)}, u32[]{:S(2)}, u32[]{:S(2)}) collective-permute-start(f32[72,128]{1,0:T(8,128)S(1)} %add.130), channel_id=1, source_target_pairs={{0,24},{4,28},{8,16},{12,20},{16,8},{20,12},{24,0},{28,4},{1,25},{... | collective-permute-start | bytes 110600 | tf_op jit(solution)/shard_map/ppermute | solution.py:407
  207.9 8.7 %collective-permute-start.93 = (f32[72,128]{1,0:T(8,128)S(1)}, f32[72,128]{1,0:T(8,128)S(1)}, u32[]{:S(2)}, u32[]{:S(2)}) collective-permute-start(f32[72,128]{1,0:T(8,128)S(1)} %add.130), channel_id=1, source_target_pairs={{0,8},{4,12},{8,0},{12,4},{16,24},{20,28},{24,16},{28,20},{1,9},{5... | collective-permute-start | bytes 110600 | tf_op jit(solution)/shard_map/ppermute | solution.py:407
  215.7 4.7 %collective-permute-start.86 = (bf16[256,128]{1,0:T(8,128)(2,1)S(1)}, bf16[256,128]{1,0:T(8,128)(2,1)S(1)}, u32[]{:S(2)}, u32[]{:S(2)}) collective-permute-start(bf16[256,128]{1,0:T(8,128)(2,1)S(1)} %get-tuple-element.333), channel_id=1, source_target_pairs={{0,8},{4,12},{8,0},{12,4},{16,24},{20,28},{24,16},{28,20},{1,9},{5... | collective-permute-start | bytes 196616 | tf_op jit(solution)/shard_map/ppermute | solution.py:407
  216.6 5.3 %collective-permute-start.96 = (f32[72,128]{1,0:T(8,128)S(1)}, f32[72,128]{1,0:T(8,128)S(1)}, u32[]{:S(2)}, u32[]{:S(2)}) collective-permute-start(f32[72,128]{1,0:T(8,128)S(1)} %add_add_fusion.2), channel_id=1, source_target_pairs={{0,1},{1,0},{2,3},{3,2},{4,5},{5,4},{6,7},{7,6},{8,9},{9,8},{10,11... | collective-permute-start | bytes 110600 | tf_op jit(solution)/shard_map/ppermute | solution.py:407
  218.1 4.8 %collective-permute-start.87 = (bf16[256,128]{1,0:T(8,128)(2,1)S(1)}, bf16[256,128]{1,0:T(8,128)(2,1)S(1)}, u32[]{:S(2)}, u32[]{:S(2)}) collective-permute-start(bf16[256,128]{1,0:T(8,128)(2,1)S(1)} %get-tuple-element.334), channel_id=1, source_target_pairs={{0,12},{4,8},{8,4},{12,0},{16,28},{20,24},{24,20},{28,16},{1,13},{... | collective-permute-start | bytes 196616 | tf_op jit(solution)/shard_map/ppermute | solution.py:407
  218.5 5.9 %collective-permute-start.88 = (bf16[256,128]{1,0:T(8,128)(2,1)S(1)}, bf16[256,128]{1,0:T(8,128)(2,1)S(1)}, u32[]{:S(2)}, u32[]{:S(2)}) collective-permute-start(bf16[256,128]{1,0:T(8,128)(2,1)S(1)} %get-tuple-element.335), channel_id=1, source_target_pairs={{0,16},{4,20},{8,24},{12,28},{16,0},{20,4},{24,8},{28,12},{1,17},{... | collective-permute-start | bytes 196616 | tf_op jit(solution)/shard_map/ppermute | solution.py:407
  219.0 5.4 %collective-permute-start.89 = (bf16[256,128]{1,0:T(8,128)(2,1)S(1)}, bf16[256,128]{1,0:T(8,128)(2,1)S(1)}, u32[]{:S(2)}, u32[]{:S(2)}) collective-permute-start(bf16[256,128]{1,0:T(8,128)(2,1)S(1)} %get-tuple-element.336), channel_id=1, source_target_pairs={{0,20},{4,16},{8,28},{12,24},{16,4},{20,0},{24,12},{28,8},{1,21},{... | collective-permute-start | bytes 196616 | tf_op jit(solution)/shard_map/ppermute | solution.py:407
  220.4 5.2 %collective-permute-start.90 = (bf16[256,128]{1,0:T(8,128)(2,1)S(1)}, bf16[256,128]{1,0:T(8,128)(2,1)S(1)}, u32[]{:S(2)}, u32[]{:S(2)}) collective-permute-start(bf16[256,128]{1,0:T(8,128)(2,1)S(1)} %get-tuple-element.337), channel_id=1, source_target_pairs={{0,24},{4,28},{8,16},{12,20},{16,8},{20,12},{24,0},{28,4},{1,25},{... | collective-permute-start | bytes 196616 | tf_op jit(solution)/shard_map/ppermute | solution.py:407
  221.8 5.2 %collective-permute-start.91 = (bf16[256,128]{1,0:T(8,128)(2,1)S(1)}, bf16[256,128]{1,0:T(8,128)(2,1)S(1)}, u32[]{:S(2)}, u32[]{:S(2)}) collective-permute-start(bf16[256,128]{1,0:T(8,128)(2,1)S(1)} %get-tuple-element.338), channel_id=1, source_target_pairs={{0,28},{4,24},{8,20},{12,16},{16,12},{20,8},{24,4},{28,0},{1,29},{... | collective-permute-start | bytes 196616 | tf_op jit(solution)/shard_map/ppermute | solution.py:407
  222.9 6.9 %collective-permute-start.97 = (f32[72,128]{1,0:T(8,128)S(1)}, f32[72,128]{1,0:T(8,128)S(1)}, u32[]{:S(2)}, u32[]{:S(2)}) collective-permute-start(f32[72,128]{1,0:T(8,128)S(1)} %add.134.refs_0_), channel_id=1, source_target_pairs={{0,2},{1,3},{2,0},{3,1},{4,6},{5,7},{6,4},{7,5},{8,10},{9,11},{10,... | collective-permute-start | bytes 110600 | tf_op jit(solution)/shard_map/ppermute | solution.py:407
  239.1 4.9 %collective-permute-start.101 = (f32[72,128]{1,0:T(8,128)S(1)}, f32[72,128]{1,0:T(8,128)S(1)}, u32[]{:S(2)}, u32[]{:S(2)}) collective-permute-start(f32[72,128]{1,0:T(8,128)S(1)} %add.135), channel_id=1, source_target_pairs={{0,24},{4,28},{8,16},{12,20},{16,8},{20,12},{24,0},{28,4},{1,25},{... | collective-permute-start | bytes 110600 | tf_op jit(solution)/shard_map/ppermute | solution.py:407
  244.3 6.8 %collective-permute-start.102 = (f32[72,128]{1,0:T(8,128)S(1)}, f32[72,128]{1,0:T(8,128)S(1)}, u32[]{:S(2)}, u32[]{:S(2)}) collective-permute-start(f32[72,128]{1,0:T(8,128)S(1)} %add_add_fusion.1.refs_0_), channel_id=1, source_target_pairs={{0,1},{1,0},{2,3},{3,2},{4,5},{5,4},{6,7},{7,6},{8,9},{9,8},{10,11... | collective-permute-start | bytes 110600 | tf_op jit(solution)/shard_map/ppermute | solution.py:407
  245.5 5.6 %collective-permute-start.103 = (f32[72,128]{1,0:T(8,128)S(1)}, f32[72,128]{1,0:T(8,128)S(1)}, u32[]{:S(2)}, u32[]{:S(2)}) collective-permute-start(f32[72,128]{1,0:T(8,128)S(1)} %add_add_fusion.1.refs_0_), channel_id=1, source_target_pairs={{0,2},{1,3},{2,0},{3,1},{4,6},{5,7},{6,4},{7,5},{8,10},{9,11},{10,... | collective-permute-start | bytes 110600 | tf_op jit(solution)/shard_map/ppermute | solution.py:407
  246.8 5.8 %collective-permute-start.104 = (f32[72,128]{1,0:T(8,128)S(1)}, f32[72,128]{1,0:T(8,128)S(1)}, u32[]{:S(2)}, u32[]{:S(2)}) collective-permute-start(f32[72,128]{1,0:T(8,128)S(1)} %add_add_fusion.1.refs_0_), channel_id=1, source_target_pairs={{0,3},{1,2},{2,1},{3,0},{4,7},{5,6},{6,5},{7,4},{8,11},{9,10},{10,... | collective-permute-start | bytes 110600 | tf_op jit(solution)/shard_map/ppermute | solution.py:407
  (34 other events, 268.7 us)

commit v2 on v1

--- a/solution.py
+++ b/solution.py
@@ -411,10 +411,9 @@
     return lax.ppermute(x, axis, [(i, (i + d) % n) for i in range(n)])
 
 
-def on_device(tiles, send_slot, slot_row, slot_fetch, fetch_list, basis):
+def prepare(tiles, send_slot, slot_row, fetch_list, basis):
     groups = lax.axis_size("rows")
     ncols = lax.axis_size("cols")
-    npts = basis.shape[0] * groups * ncols
     sums, stay, leads = lead(tiles, send_slot, ncols)
     rests = rest(tiles, send_slot, ncols, leads[0])
     wish = later(fetch_list, rests[0])
@@ -423,6 +422,14 @@
     chunks = [stay, *leads, *rests]
     lists = [wish] + [swap(wish, "rows", groups, d) for d in range(1, groups)]
     scale, asked, out = start(slot_row, lists, [sums, *leads], basis)
+    return chunks, scale, asked, out
+
+
+def on_device(tiles, send_slot, slot_row, slot_fetch, fetch_list, basis):
+    groups = lax.axis_size("rows")
+    ncols = lax.axis_size("cols")
+    npts = basis.shape[0] * groups * ncols
+    chunks, scale, asked, out = prepare(tiles, send_slot, slot_row, fetch_list, basis)
     stages = [("rows", groups, [1])]
     bit = 2
     while bit < groups:
@@ -441,7 +448,7 @@
     def fetched(out):
         return [out[0]] + [swap(out[d], "rows", groups, d) for d in range(1, groups)]
 
-    first_out, growth = out, []
+    growth = []
     parts = before = None
     for k in range(ITERS):
         last = k == ITERS - 1
@@ -457,16 +464,17 @@
     gram, y = res
     fast = finish(total(gram, at_once), y, npts)
 
-    def repeat(k, state):
-        gram, y = step(slot_row, slot_fetch, asked, scale, chunks, fetched(state[1]), False, False)
-        v, out = careful(asked, total(gram, apart), scale, y, npts)
-        return v, tuple(out)
-
-    return lax.cond(
-        sum(growth) < GROWTH,
-        lambda: fast,
-        lambda: lax.fori_loop(0, ITERS, repeat, (fast, tuple(first_out)))[0],
-    )
+    def again():
+        chunks, scale, asked, out = prepare(tiles, send_slot, slot_row, fetch_list, basis)
+
+        def repeat(k, state):
+            gram, y = step(slot_row, slot_fetch, asked, scale, chunks, fetched(state[1]), False, False)
+            v, out = careful(asked, total(gram, apart), scale, y, npts)
+            return v, tuple(out)
+
+        return lax.fori_loop(0, ITERS, repeat, (basis, tuple(out)))[0]
+
+    return lax.cond(sum(growth) < GROWTH, lambda: fast, again)
 
 
 def solution(mesh):

time: 261 us -> 258 us (0.989)
  starting transfers between devices: 111 us -> 131 us
  waiting for transfers between devices: 78.8 us -> 59.6 us
  Pallas kernels: 62.3 us -> 58.9 us
    ppermute x6, waiting for transfers between devices: 37.2 us -> 19.1 us  [shift(): return lax.ppermute(x, axis, [(i, (i + d) % n) for i in range(n)])]
    ppermute x86, starting transfers between devices: 100 us -> 112 us  [swap(): return lax.ppermute(x, axis, [(i, i ^ d) for i in range(n)])]
    ppermute x6, starting transfers between devices: 11.2 us -> 18.5 us  [shift(): return lax.ppermute(x, axis, [(i, (i + d) % n) for i in range(n)])]
    pallas_call x6, Pallas kernels: 18.8 us -> 14.3 us  [step(): pl.pallas_call(functools.partial(step_kernel, ncols, groups, first, last)...]
  transfers between devices with their start and end apart: 92 -> 92, of which waited for: 35 -> 37; matrix products, arithmetic and copies ran while one was open for 0% -> 0% of each run, Pallas kernels for 17% -> 16%
where the time goes in v2:
time: 258 us; the launch traced here: 255 us
  starting transfers between devices  131 us (51%)
  waiting for transfers between devices  59.6 us (23%)
  Pallas kernels  58.9 us (23%)
  local copies, waits for them, and re-layouts  3.76 us (1%)
    ppermute x86, starting transfers between devices, swap(): return lax.ppermute(x, axis, [(i, i ^ d) for i in range(n)])  112 us
    ppermute x86, waiting for transfers between devices, swap(): return lax.ppermute(x, axis, [(i, i ^ d) for i in range(n)])  40.5 us
    pallas_call x5, Pallas kernels, turn(): pl.pallas_call(functools.partial(turn_kernel, npts, groups, len(parts), f...  31.4 us
    ppermute x6, waiting for transfers between devices, shift(): return lax.ppermute(x, axis, [(i, (i + d) % n) for i in range(n)])  19.1 us
    ppermute x6, starting transfers between devices, shift(): return lax.ppermute(x, axis, [(i, (i + d) % n) for i in range(n)])  18.5 us
    pallas_call x6, Pallas kernels, step(): pl.pallas_call(functools.partial(step_kernel, ncols, groups, first, last)...  14.3 us
    pallas_call x1, Pallas kernels, finish(): pl.pallas_call(functools.partial(finish_kernel, npts, len(parts)), out_sh...  5.68 us
  transfers between devices with their start and end apart: 92, of which 37 were waited for; matrix products, arithmetic and copies ran while one was open for 0% of the time, Pallas kernels for 16%

profile of v2, /device:TPU:0, one launch (start us, length us, event | category | flops | bytes accessed | tf_op | source)
XLA Modules:
  0.0 255.2 jit_solution(6938787035997942383)
XLA Ops:
  1.1 4.2 %shard_map.66 = (f32[8,256]{1,0:T(8,128)S(1)}, bf16[8,256,256]{2,1,0:T(8,128)(2,1)S(1)}, bf16[800,256]{1,0:T(8,128)(2,1)S(1)}, bf16[800,256]{1,0:T(8,128)(2,1)S(1)}, bf16[800,256]{1,0:T(8,128)(2,1)S(1)}) custom-call(s32[1,32]{1,0:T(1,128)} %send_ref.3, bf16[32,256,256]{2,1,0:T(8,128)(2,1)} %tiles_ref.3), custom_call_target="tpu_custom_call" | custom-call | tf_op jit(solution)/shard_map/pallas_call | solution.py:67
  5.2 4.1 %collective-permute-start.34 = (bf16[800,256]{1,0:T(8,128)(2,1)S(1)}, bf16[800,256]{1,0:T(8,128)(2,1)S(1)}, u32[]{:S(2)}, u32[]{:S(2)}) collective-permute-start(bf16[800,256]{1,0:T(8,128)(2,1)S(1)} %get-tuple-element.244), channel_id=1, source_target_pairs={{0,2},{1,3},{2,0},{3,1},{4,6},{5,7},{6,4},{7,5},{8,10},{9,11},{10,... | collective-permute-start | bytes 1228808 | tf_op jit(solution)/shard_map/ppermute | solution.py:411
  14.6 1.5 collective-permute-start.31
  17.6 1.5 collective-permute-done.31.refs_6_
  24.2 2.0 collective-permute-done.27.refs_2_
  27.5 2.6 %collective-permute-start.38 = (bf16[5,256,256]{2,1,0:T(8,128)(2,1)S(1)}, bf16[5,256,256]{2,1,0:T(8,128)(2,1)S(1)}, u32[]{:S(2)}, u32[]{:S(2)}) collective-permute-start(bf16[5,256,256]{2,1,0:T(8,128)(2,1)S(1)} %get-tuple-element.250), channel_id=1, source_target_pairs={{0,3},{1,0},{2,1},{3,2},{4,7},{5,4},{6,5},{7,6},{8,11},{9,8},{10,9... | collective-permute-start | bytes 1966088 | tf_op jit(solution)/shard_map/ppermute | solution.py:411
  30.1 8.4 %collective-permute-start.36 = (bf16[5,256,256]{2,1,0:T(8,128)(2,1)S(1)}, bf16[5,256,256]{2,1,0:T(8,128)(2,1)S(1)}, u32[]{:S(2)}, u32[]{:S(2)}) collective-permute-start(bf16[5,256,256]{2,1,0:T(8,128)(2,1)S(1)} %get-tuple-element.242.after_ref), channel_id=1, source_target_pairs={{0,1},{1,2},{2,3},{3,0},{4,5},{5,6},{6,7},{7,4},{8,9},{9,10},{10,1... | collective-permute-start | bytes 1966088 | tf_op jit(solution)/shard_map/ppermute | solution.py:411
  40.1 14.0 %collective-permute-start.40 = (bf16[256,128]{1,0:T(8,128)(2,1)S(1)}, bf16[256,128]{1,0:T(8,128)(2,1)S(1)}, u32[]{:S(2)}, u32[]{:S(2)}) collective-permute-start(bf16[256,128]{1,0:T(8,128)(2,1)S(1)} %get-tuple-element.253), channel_id=1, source_target_pairs={{0,8},{4,12},{8,0},{12,4},{16,24},{20,28},{24,16},{28,20},{1,9},{5... | collective-permute-start | bytes 196616 | tf_op jit(solution)/shard_map/ppermute | solution.py:407
  55.0 1.7 collective-permute-done.40.refs_9_
  56.7 1.8 collective-permute-start.42
  59.4 1.6 collective-permute-done.42.refs_11_
  61.0 3.6 %collective-permute-start.44 = (bf16[256,128]{1,0:T(8,128)(2,1)S(1)}, bf16[256,128]{1,0:T(8,128)(2,1)S(1)}, u32[]{:S(2)}, u32[]{:S(2)}) collective-permute-start(bf16[256,128]{1,0:T(8,128)(2,1)S(1)} %get-tuple-element.257), channel_id=1, source_target_pairs={{0,24},{4,28},{8,16},{12,20},{16,8},{20,12},{24,0},{28,4},{1,25},{... | collective-permute-start | bytes 196616 | tf_op jit(solution)/shard_map/ppermute | solution.py:407
  65.2 1.7 collective-permute-done.44.refs_13_
  66.8 2.4 collective-permute-done.45.refs_14_
  69.2 19.0 %collective-permute-done.37.refs_5_ = bf16[5,256,256]{2,1,0:T(8,128)(2,1)S(1)} collective-permute-done((bf16[5,256,256]{2,1,0:T(8,128)(2,1)S(1)}, bf16[5,256,256]{2,1,0:T(8,128)(2,1)S(1)}, u32[]{:S(2)}, u32[]{:S(2)}) %collective-permute-start.37) | collective-permute-done | bytes 655392 | tf_op jit(solution)/shard_map/ppermute | solution.py:411
  88.2 2.4 shard_map.70
  91.9 2.8 %collective-permute-start.56 = (f32[72,128]{1,0:T(8,128)S(1)}, f32[72,128]{1,0:T(8,128)S(1)}, u32[]{:S(2)}, u32[]{:S(2)}) collective-permute-start(f32[72,128]{1,0:T(8,128)S(1)} %add.109), channel_id=1, source_target_pairs={{0,24},{4,28},{8,16},{12,20},{16,8},{20,12},{24,0},{28,4},{1,25},{... | collective-permute-start | bytes 110600 | tf_op jit(solution)/shard_map/ppermute | solution.py:407
  95.4 1.8 collective-permute-start.47
  97.2 1.4 collective-permute-done.55
  99.6 13.5 %collective-permute-start.57 = (f32[72,128]{1,0:T(8,128)S(1)}, f32[72,128]{1,0:T(8,128)S(1)}, u32[]{:S(2)}, u32[]{:S(2)}) collective-permute-start(f32[72,128]{1,0:T(8,128)S(1)} %add_add_fusion.6), channel_id=1, source_target_pairs={{0,1},{1,0},{2,3},{3,2},{4,5},{5,4},{6,7},{7,6},{8,9},{9,8},{10,11... | collective-permute-start | bytes 110600 | tf_op jit(solution)/shard_map/ppermute | solution.py:407
  113.1 1.5 collective-permute-start.49
  114.8 2.8 %collective-permute-start.51 = (bf16[256,128]{1,0:T(8,128)(2,1)S(1)}, bf16[256,128]{1,0:T(8,128)(2,1)S(1)}, u32[]{:S(2)}, u32[]{:S(2)}) collective-permute-start(bf16[256,128]{1,0:T(8,128)(2,1)S(1)} %get-tuple-element.265), channel_id=1, source_target_pairs={{0,24},{4,28},{8,16},{12,20},{16,8},{20,12},{24,0},{28,4},{1,25},{... | collective-permute-start | bytes 196616 | tf_op jit(solution)/shard_map/ppermute | solution.py:407
  117.6 2.1 collective-permute-start.58
  120.3 1.9 collective-permute-done.52.refs_14_
  122.2 2.4 shard_map.71
  124.7 5.9 %shard_map.72 = (f32[128,128]{1,0:T(8,128)S(1)}, f32[128,128]{1,0:T(8,128)S(1)}, f32[8,128]{1,0:T(8,128)}, bf16[256,128]{1,0:T(8,128)(2,1)S(1)}, bf16[256,128]{1...) custom-call(s32[1,8]{1,0:T(1,128)S(1)} %get-tuple-element.246.asked_, ...), custom_call_target="tpu_custom_call" | custom-call | tf_op jit(solution)/shard_map/pallas_call | solution.py:294
  131.9 1.8 collective-permute-start.69
  135.4 1.4 collective-permute-done.69
  143.2 1.7 collective-permute-done.64.refs_13_
  145.9 2.6 %shard_map.73 = (f32[72,128]{1,0:T(8,128)S(1)}, f32[512,128]{1,0:T(8,128)S(1)}) custom-call(s32[1,32]{1,0:T(1,128)S(1)} %copy-done.2, s32[1,32]{1,0:T(1,128)S(1)} %copy-done.3, s32[1,8]{1,0:T(1,128)S(1)} %get-tuple-element.246.asked_ref, f32[512,128]{1,0:T(8,128)S(1)} %get-tuple-element.247.scale_ref, bf16[8,256,256]{2,1,0:T(8,128)(2,1)S(1)} %get-tuple-element.248.refs_0_, ...), custom_call_target="tpu_custom_call" | custom-call | tf_op jit(solution)/shard_map/pallas_call | solution.py:227
  148.9 2.2 collective-permute-start.71
  151.1 1.4 collective-permute-start.82
  154.7 6.3 %shard_map.74 = (f32[128,128]{1,0:T(8,128)S(1)}, f32[128,128]{1,0:T(8,128)S(1)}, f32[8,128]{1,0:T(8,128)S(1)}, bf16[256,128]{1,0:T(8,128)(2,1)S(1)}, bf16[256,12...) custom-call(s32[1,8]{1,0:T(1,128)S(1)} %get-tuple-element.246.asked_, ...), custom_call_target="tpu_custom_call" | custom-call | tf_op jit(solution)/shard_map/pallas_call | solution.py:294
  162.3 1.9 collective-permute-start.83
  164.6 1.7 collective-permute-start.75
  166.5 1.5 collective-permute-start.77
  169.0 1.6 collective-permute-start.84
  170.5 2.1 collective-permute-done.76.refs_12_
  173.1 2.4 shard_map.75
  175.7 6.1 %shard_map.76 = (f32[128,128]{1,0:T(8,128)S(1)}, f32[128,128]{1,0:T(8,128)S(1)}, f32[8,128]{1,0:T(8,128)}, bf16[256,128]{1,0:T(8,128)(2,1)S(1)}, bf16[256,128]{1...) custom-call(s32[1,8]{1,0:T(1,128)S(1)} %get-tuple-element.246.asked_, ...), custom_call_target="tpu_custom_call" | custom-call | tf_op jit(solution)/shard_map/pallas_call | solution.py:294
  182.3 1.8 collective-permute-start.86
  185.9 1.8 collective-permute-start.93
  187.7 1.6 collective-permute-done.95
  191.2 1.8 collective-permute-start.90
  195.3 1.7 collective-permute-done.90.refs_13_
  197.9 2.4 shard_map.77
  200.7 1.6 collective-permute-start.97
  202.3 1.8 collective-permute-start.108
  206.0 6.3 %shard_map.78 = (f32[128,128]{1,0:T(8,128)S(1)}, f32[128,128]{1,0:T(8,128)S(1)}, f32[8,128]{1,0:T(8,128)S(1)}, bf16[256,128]{1,0:T(8,128)(2,1)S(1)}, bf16[256,12...) custom-call(s32[1,8]{1,0:T(1,128)S(1)} %get-tuple-element.246.asked_, ...), custom_call_target="tpu_custom_call" | custom-call | tf_op jit(solution)/shard_map/pallas_call | solution.py:294
  212.4 1.5 collective-permute-start.99
  214.9 1.4 collective-permute-start.101
  216.9 1.7 collective-permute-start.103
  219.3 1.9 collective-permute-start.110
  222.1 1.6 collective-permute-done.104.refs_14_
  223.7 2.0 shard_map.79.p_ref
  225.7 6.8 %shard_map.80 = (f32[72,128]{1,0:T(8,128)S(1)}, f32[512,128]{1,0:T(8,128)S(1)}) custom-call(s32[1,8]{1,0:T(1,128)S(1)} %get-tuple-element.246.asked_ref, f32[512,128]{1,0:T(8,128)S(1)} %get-tuple-element.247.scale_ref, f32[512,128]{1,0:T(8,128)S(1)} %shard_map.79.p_ref, f32[72,128]{1,0:T(8,128)S(1)} %add.134.refs_0_, ...), custom_call_target="tpu_custom_call" | custom-call | tf_op jit(solution)/shard_map/pallas_call | solution.py:294
  235.2 1.5 collective-permute-start.113
  237.3 1.4 collective-permute-done.114
  239.1 1.5 collective-permute-done.112
  240.6 2.2 collective-permute-start.117
  243.4 1.7 collective-permute-start.115
  247.8 5.7 %shard_map.81 = bf16[512,128]{1,0:T(8,128)(2,1)} custom-call(f32[512,128]{1,0:T(8,128)S(1)} %get-tuple-element.318.y_ref, f32[72,128]{1,0:T(8,128)S(1)} %add_add_fusion.1.refs_0_, f32[72,128]{1,0:T(8,128)S(1)} %collective-permute-done.115.refs_1_, f32[72,128]{1,0:T(8,128)S(1)} %collective-permute-done.116.refs_2_, f32[72,128]{1,0:T(8,128)S(1)} %collective-permute-done.117.refs_3_), custom_call_target="tpu_custom_call" | custom-call | tf_op jit(solution)/shard_map/pallas_call | solution.py:396
  253.4 1.6 conditional.1
  253.4 1.6 copy.40
  (170 shorter events, 57.2 us)
Async XLA Ops:
  5.2 24.9 %collective-permute-start.34 = (bf16[800,256]{1,0:T(8,128)(2,1)S(1)}, bf16[800,256]{1,0:T(8,128)(2,1)S(1)}, u32[]{:S(2)}, u32[]{:S(2)}) collective-permute-start(bf16[800,256]{1,0:T(8,128)(2,1)S(1)} %get-tuple-element.244), channel_id=1, source_target_pairs={{0,2},{1,3},{2,0},{3,1},{4,6},{5,7},{6,4},{7,5},{8,10},{9,11},{10,... | collective-permute-start | bytes 1228808 | tf_op jit(solution)/shard_map/ppermute | solution.py:411
  9.4 29.2 %collective-permute-start.35 = (bf16[800,256]{1,0:T(8,128)(2,1)S(1)}, bf16[800,256]{1,0:T(8,128)(2,1)S(1)}, u32[]{:S(2)}, u32[]{:S(2)}) collective-permute-start(bf16[800,256]{1,0:T(8,128)(2,1)S(1)} %get-tuple-element.245), channel_id=1, source_target_pairs={{0,3},{1,0},{2,1},{3,2},{4,7},{5,4},{6,5},{7,6},{8,11},{9,8},{10,9... | collective-permute-start | bytes 1228808 | tf_op jit(solution)/shard_map/ppermute | solution.py:411
  10.7 28.0 %collective-permute-start.33 = (bf16[800,256]{1,0:T(8,128)(2,1)S(1)}, bf16[800,256]{1,0:T(8,128)(2,1)S(1)}, u32[]{:S(2)}, u32[]{:S(2)}) collective-permute-start(bf16[800,256]{1,0:T(8,128)(2,1)S(1)} %get-tuple-element.241.after_ref), channel_id=1, source_target_pairs={{0,1},{1,2},{2,3},{3,0},{4,5},{5,6},{6,7},{7,4},{8,9},{9,10},{10,1... | collective-permute-start | bytes 1228808 | tf_op jit(solution)/shard_map/ppermute | solution.py:411
  26.2 62.0 %collective-permute-start.37 = (bf16[5,256,256]{2,1,0:T(8,128)(2,1)S(1)}, bf16[5,256,256]{2,1,0:T(8,128)(2,1)S(1)}, u32[]{:S(2)}, u32[]{:S(2)}) collective-permute-start(bf16[5,256,256]{2,1,0:T(8,128)(2,1)S(1)} %get-tuple-element.249), channel_id=1, source_target_pairs={{0,2},{1,3},{2,0},{3,1},{4,6},{5,7},{6,4},{7,5},{8,10},{9,11},{10,... | collective-permute-start | bytes 1966088 | tf_op jit(solution)/shard_map/ppermute | solution.py:411
  27.5 60.7 %collective-permute-start.38 = (bf16[5,256,256]{2,1,0:T(8,128)(2,1)S(1)}, bf16[5,256,256]{2,1,0:T(8,128)(2,1)S(1)}, u32[]{:S(2)}, u32[]{:S(2)}) collective-permute-start(bf16[5,256,256]{2,1,0:T(8,128)(2,1)S(1)} %get-tuple-element.250), channel_id=1, source_target_pairs={{0,3},{1,0},{2,1},{3,2},{4,7},{5,4},{6,5},{7,6},{8,11},{9,8},{10,9... | collective-permute-start | bytes 1966088 | tf_op jit(solution)/shard_map/ppermute | solution.py:411
  30.1 58.0 %collective-permute-start.36 = (bf16[5,256,256]{2,1,0:T(8,128)(2,1)S(1)}, bf16[5,256,256]{2,1,0:T(8,128)(2,1)S(1)}, u32[]{:S(2)}, u32[]{:S(2)}) collective-permute-start(bf16[5,256,256]{2,1,0:T(8,128)(2,1)S(1)} %get-tuple-element.242.after_ref), channel_id=1, source_target_pairs={{0,1},{1,2},{2,3},{3,0},{4,5},{5,6},{6,7},{7,4},{8,9},{9,10},{10,1... | collective-permute-start | bytes 1966088 | tf_op jit(solution)/shard_map/ppermute | solution.py:411
  40.0 14.1 %collective-permute-start.39 = (bf16[256,128]{1,0:T(8,128)(2,1)S(1)}, bf16[256,128]{1,0:T(8,128)(2,1)S(1)}, u32[]{:S(2)}, u32[]{:S(2)}) collective-permute-start(bf16[256,128]{1,0:T(8,128)(2,1)S(1)} %get-tuple-element.252), channel_id=1, source_target_pairs={{0,4},{4,0},{8,12},{12,8},{16,20},{20,16},{24,28},{28,24},{1,5},{5... | collective-permute-start | bytes 196616 | tf_op jit(solution)/shard_map/ppermute | solution.py:407
  40.1 16.7 %collective-permute-start.40 = (bf16[256,128]{1,0:T(8,128)(2,1)S(1)}, bf16[256,128]{1,0:T(8,128)(2,1)S(1)}, u32[]{:S(2)}, u32[]{:S(2)}) collective-permute-start(bf16[256,128]{1,0:T(8,128)(2,1)S(1)} %get-tuple-element.253), channel_id=1, source_target_pairs={{0,8},{4,12},{8,0},{12,4},{16,24},{20,28},{24,16},{28,20},{1,9},{5... | collective-permute-start | bytes 196616 | tf_op jit(solution)/shard_map/ppermute | solution.py:407
  58.5 6.1 %collective-permute-start.43 = (bf16[256,128]{1,0:T(8,128)(2,1)S(1)}, bf16[256,128]{1,0:T(8,128)(2,1)S(1)}, u32[]{:S(2)}, u32[]{:S(2)}) collective-permute-start(bf16[256,128]{1,0:T(8,128)(2,1)S(1)} %get-tuple-element.256), channel_id=1, source_target_pairs={{0,20},{4,16},{8,28},{12,24},{16,4},{20,0},{24,12},{28,8},{1,21},{... | collective-permute-start | bytes 196616 | tf_op jit(solution)/shard_map/ppermute | solution.py:407
  61.0 5.8 %collective-permute-start.44 = (bf16[256,128]{1,0:T(8,128)(2,1)S(1)}, bf16[256,128]{1,0:T(8,128)(2,1)S(1)}, u32[]{:S(2)}, u32[]{:S(2)}) collective-permute-start(bf16[256,128]{1,0:T(8,128)(2,1)S(1)} %get-tuple-element.257), channel_id=1, source_target_pairs={{0,24},{4,28},{8,16},{12,20},{16,8},{20,12},{24,0},{28,4},{1,25},{... | collective-permute-start | bytes 196616 | tf_op jit(solution)/shard_map/ppermute | solution.py:407
  91.9 5.3 %collective-permute-start.56 = (f32[72,128]{1,0:T(8,128)S(1)}, f32[72,128]{1,0:T(8,128)S(1)}, u32[]{:S(2)}, u32[]{:S(2)}) collective-permute-start(f32[72,128]{1,0:T(8,128)S(1)} %add.109), channel_id=1, source_target_pairs={{0,24},{4,28},{8,16},{12,20},{16,8},{20,12},{24,0},{28,4},{1,25},{... | collective-permute-start | bytes 110600 | tf_op jit(solution)/shard_map/ppermute | solution.py:407
  95.4 19.3 %collective-permute-start.46 = (bf16[256,128]{1,0:T(8,128)(2,1)S(1)}, bf16[256,128]{1,0:T(8,128)(2,1)S(1)}, u32[]{:S(2)}, u32[]{:S(2)}) collective-permute-start(bf16[256,128]{1,0:T(8,128)(2,1)S(1)} %get-tuple-element.260), channel_id=1, source_target_pairs={{0,4},{4,0},{8,12},{12,8},{16,20},{20,16},{24,28},{28,24},{1,5},{5... | collective-permute-start | bytes 196616 | tf_op jit(solution)/shard_map/ppermute | solution.py:407
  95.4 19.4 %collective-permute-start.47 = (bf16[256,128]{1,0:T(8,128)(2,1)S(1)}, bf16[256,128]{1,0:T(8,128)(2,1)S(1)}, u32[]{:S(2)}, u32[]{:S(2)}) collective-permute-start(bf16[256,128]{1,0:T(8,128)(2,1)S(1)} %get-tuple-element.261), channel_id=1, source_target_pairs={{0,8},{4,12},{8,0},{12,4},{16,24},{20,28},{24,16},{28,20},{1,9},{5... | collective-permute-start | bytes 196616 | tf_op jit(solution)/shard_map/ppermute | solution.py:407
  99.6 18.0 %collective-permute-start.57 = (f32[72,128]{1,0:T(8,128)S(1)}, f32[72,128]{1,0:T(8,128)S(1)}, u32[]{:S(2)}, u32[]{:S(2)}) collective-permute-start(f32[72,128]{1,0:T(8,128)S(1)} %add_add_fusion.6), channel_id=1, source_target_pairs={{0,1},{1,0},{2,3},{3,2},{4,5},{5,4},{6,7},{7,6},{8,9},{9,8},{10,11... | collective-permute-start | bytes 110600 | tf_op jit(solution)/shard_map/ppermute | solution.py:407
  113.1 6.6 %collective-permute-start.49 = (bf16[256,128]{1,0:T(8,128)(2,1)S(1)}, bf16[256,128]{1,0:T(8,128)(2,1)S(1)}, u32[]{:S(2)}, u32[]{:S(2)}) collective-permute-start(bf16[256,128]{1,0:T(8,128)(2,1)S(1)} %get-tuple-element.263), channel_id=1, source_target_pairs={{0,16},{4,20},{8,24},{12,28},{16,0},{20,4},{24,8},{28,12},{1,17},{... | collective-permute-start | bytes 196616 | tf_op jit(solution)/shard_map/ppermute | solution.py:407
  114.7 5.0 %collective-permute-start.50 = (bf16[256,128]{1,0:T(8,128)(2,1)S(1)}, bf16[256,128]{1,0:T(8,128)(2,1)S(1)}, u32[]{:S(2)}, u32[]{:S(2)}) collective-permute-start(bf16[256,128]{1,0:T(8,128)(2,1)S(1)} %get-tuple-element.264), channel_id=1, source_target_pairs={{0,20},{4,16},{8,28},{12,24},{16,4},{20,0},{24,12},{28,8},{1,21},{... | collective-permute-start | bytes 196616 | tf_op jit(solution)/shard_map/ppermute | solution.py:407
  114.8 5.5 %collective-permute-start.51 = (bf16[256,128]{1,0:T(8,128)(2,1)S(1)}, bf16[256,128]{1,0:T(8,128)(2,1)S(1)}, u32[]{:S(2)}, u32[]{:S(2)}) collective-permute-start(bf16[256,128]{1,0:T(8,128)(2,1)S(1)} %get-tuple-element.265), channel_id=1, source_target_pairs={{0,24},{4,28},{8,16},{12,20},{16,8},{20,12},{24,0},{28,4},{1,25},{... | collective-permute-start | bytes 196616 | tf_op jit(solution)/shard_map/ppermute | solution.py:407
  117.6 7.1 %collective-permute-start.58 = (f32[72,128]{1,0:T(8,128)S(1)}, f32[72,128]{1,0:T(8,128)S(1)}, u32[]{:S(2)}, u32[]{:S(2)}) collective-permute-start(f32[72,128]{1,0:T(8,128)S(1)} %add.113.refs_0_), channel_id=1, source_target_pairs={{0,2},{1,3},{2,0},{3,1},{4,6},{5,7},{6,4},{7,5},{8,10},{9,11},{10,... | collective-permute-start | bytes 110600 | tf_op jit(solution)/shard_map/ppermute | solution.py:407
  124.6 7.2 %collective-permute-start.66 = (f32[72,128]{1,0:T(8,128)S(1)}, f32[72,128]{1,0:T(8,128)S(1)}, u32[]{:S(2)}, u32[]{:S(2)}) collective-permute-start(f32[72,128]{1,0:T(8,128)S(1)} %get-tuple-element.278), channel_id=1, source_target_pairs={{0,4},{4,0},{8,12},{12,8},{16,20},{20,16},{24,28},{28,24},{1,5},{5... | collective-permute-start | bytes 110600 | tf_op jit(solution)/shard_map/ppermute | solution.py:407
  130.6 9.0 %collective-permute-start.59 = (bf16[256,128]{1,0:T(8,128)(2,1)S(1)}, bf16[256,128]{1,0:T(8,128)(2,1)S(1)}, u32[]{:S(2)}, u32[]{:S(2)}) collective-permute-start(bf16[256,128]{1,0:T(8,128)(2,1)S(1)} %get-tuple-element.270), channel_id=1, source_target_pairs={{0,4},{4,0},{8,12},{12,8},{16,20},{20,16},{24,28},{28,24},{1,5},{5... | collective-permute-start | bytes 196616 | tf_op jit(solution)/shard_map/ppermute | solution.py:407
  131.1 9.7 %collective-permute-start.60 = (bf16[256,128]{1,0:T(8,128)(2,1)S(1)}, bf16[256,128]{1,0:T(8,128)(2,1)S(1)}, u32[]{:S(2)}, u32[]{:S(2)}) collective-permute-start(bf16[256,128]{1,0:T(8,128)(2,1)S(1)} %get-tuple-element.271), channel_id=1, source_target_pairs={{0,8},{4,12},{8,0},{12,4},{16,24},{20,28},{24,16},{28,20},{1,9},{5... | collective-permute-start | bytes 196616 | tf_op jit(solution)/shard_map/ppermute | solution.py:407
  131.9 4.9 %collective-permute-start.69 = (f32[72,128]{1,0:T(8,128)S(1)}, f32[72,128]{1,0:T(8,128)S(1)}, u32[]{:S(2)}, u32[]{:S(2)}) collective-permute-start(f32[72,128]{1,0:T(8,128)S(1)} %add.114), channel_id=1, source_target_pairs={{0,24},{4,28},{8,16},{12,20},{16,8},{20,12},{24,0},{28,4},{1,25},{... | collective-permute-start | bytes 110600 | tf_op jit(solution)/shard_map/ppermute | solution.py:407
  136.8 5.3 %collective-permute-start.61 = (bf16[256,128]{1,0:T(8,128)(2,1)S(1)}, bf16[256,128]{1,0:T(8,128)(2,1)S(1)}, u32[]{:S(2)}, u32[]{:S(2)}) collective-permute-start(bf16[256,128]{1,0:T(8,128)(2,1)S(1)} %get-tuple-element.272), channel_id=1, source_target_pairs={{0,12},{4,8},{8,4},{12,0},{16,28},{20,24},{24,20},{28,16},{1,13},{... | collective-permute-start | bytes 196616 | tf_op jit(solution)/shard_map/ppermute | solution.py:407
  137.7 4.9 %collective-permute-start.62 = (bf16[256,128]{1,0:T(8,128)(2,1)S(1)}, bf16[256,128]{1,0:T(8,128)(2,1)S(1)}, u32[]{:S(2)}, u32[]{:S(2)}) collective-permute-start(bf16[256,128]{1,0:T(8,128)(2,1)S(1)} %get-tuple-element.273), channel_id=1, source_target_pairs={{0,16},{4,20},{8,24},{12,28},{16,0},{20,4},{24,8},{28,12},{1,17},{... | collective-permute-start | bytes 196616 | tf_op jit(solution)/shard_map/ppermute | solution.py:407
  139.5 5.4 %collective-permute-start.64 = (bf16[256,128]{1,0:T(8,128)(2,1)S(1)}, bf16[256,128]{1,0:T(8,128)(2,1)S(1)}, u32[]{:S(2)}, u32[]{:S(2)}) collective-permute-start(bf16[256,128]{1,0:T(8,128)(2,1)S(1)} %get-tuple-element.275), channel_id=1, source_target_pairs={{0,24},{4,28},{8,16},{12,20},{16,8},{20,12},{24,0},{28,4},{1,25},{... | collective-permute-start | bytes 196616 | tf_op jit(solution)/shard_map/ppermute | solution.py:407
  140.8 5.2 %collective-permute-start.65 = (bf16[256,128]{1,0:T(8,128)(2,1)S(1)}, bf16[256,128]{1,0:T(8,128)(2,1)S(1)}, u32[]{:S(2)}, u32[]{:S(2)}) collective-permute-start(bf16[256,128]{1,0:T(8,128)(2,1)S(1)} %get-tuple-element.276), channel_id=1, source_target_pairs={{0,28},{4,24},{8,20},{12,16},{16,12},{20,8},{24,4},{28,0},{1,29},{... | collective-permute-start | bytes 196616 | tf_op jit(solution)/shard_map/ppermute | solution.py:407
  142.1 6.8 %collective-permute-start.70 = (f32[72,128]{1,0:T(8,128)S(1)}, f32[72,128]{1,0:T(8,128)S(1)}, u32[]{:S(2)}, u32[]{:S(2)}) collective-permute-start(f32[72,128]{1,0:T(8,128)S(1)} %add_add_fusion.5), channel_id=1, source_target_pairs={{0,1},{1,0},{2,3},{3,2},{4,5},{5,4},{6,7},{7,6},{8,9},{9,8},{10,11... | collective-permute-start | bytes 110600 | tf_op jit(solution)/shard_map/ppermute | solution.py:407
  148.9 5.8 %collective-permute-start.71 = (f32[72,128]{1,0:T(8,128)S(1)}, f32[72,128]{1,0:T(8,128)S(1)}, u32[]{:S(2)}, u32[]{:S(2)}) collective-permute-start(f32[72,128]{1,0:T(8,128)S(1)} %add.118.refs_0_), channel_id=1, source_target_pairs={{0,2},{1,3},{2,0},{3,1},{4,6},{5,7},{6,4},{7,5},{8,10},{9,11},{10,... | collective-permute-start | bytes 110600 | tf_op jit(solution)/shard_map/ppermute | solution.py:407
  151.1 11.1 %collective-permute-start.82 = (f32[72,128]{1,0:T(8,128)S(1)}, f32[72,128]{1,0:T(8,128)S(1)}, u32[]{:S(2)}, u32[]{:S(2)}) collective-permute-start(f32[72,128]{1,0:T(8,128)S(1)} %add.119), channel_id=1, source_target_pairs={{0,24},{4,28},{8,16},{12,20},{16,8},{20,12},{24,0},{28,4},{1,25},{... | collective-permute-start | bytes 110600 | tf_op jit(solution)/shard_map/ppermute | solution.py:407
  152.5 9.8 %collective-permute-start.81 = (f32[72,128]{1,0:T(8,128)S(1)}, f32[72,128]{1,0:T(8,128)S(1)}, u32[]{:S(2)}, u32[]{:S(2)}) collective-permute-start(f32[72,128]{1,0:T(8,128)S(1)} %add.119), channel_id=1, source_target_pairs={{0,16},{4,20},{8,24},{12,28},{16,0},{20,4},{24,8},{28,12},{1,17},{... | collective-permute-start | bytes 110600 | tf_op jit(solution)/shard_map/ppermute | solution.py:407
  153.7 8.5 %collective-permute-start.80 = (f32[72,128]{1,0:T(8,128)S(1)}, f32[72,128]{1,0:T(8,128)S(1)}, u32[]{:S(2)}, u32[]{:S(2)}) collective-permute-start(f32[72,128]{1,0:T(8,128)S(1)} %add.119), channel_id=1, source_target_pairs={{0,8},{4,12},{8,0},{12,4},{16,24},{20,28},{24,16},{28,20},{1,9},{5... | collective-permute-start | bytes 110600 | tf_op jit(solution)/shard_map/ppermute | solution.py:407
  161.0 5.3 %collective-permute-start.72 = (bf16[256,128]{1,0:T(8,128)(2,1)S(1)}, bf16[256,128]{1,0:T(8,128)(2,1)S(1)}, u32[]{:S(2)}, u32[]{:S(2)}) collective-permute-start(bf16[256,128]{1,0:T(8,128)(2,1)S(1)} %get-tuple-element.283), channel_id=1, source_target_pairs={{0,4},{4,0},{8,12},{12,8},{16,20},{20,16},{24,28},{28,24},{1,5},{5... | collective-permute-start | bytes 196616 | tf_op jit(solution)/shard_map/ppermute | solution.py:407
  161.0 5.5 %collective-permute-start.73 = (bf16[256,128]{1,0:T(8,128)(2,1)S(1)}, bf16[256,128]{1,0:T(8,128)(2,1)S(1)}, u32[]{:S(2)}, u32[]{:S(2)}) collective-permute-start(bf16[256,128]{1,0:T(8,128)(2,1)S(1)} %get-tuple-element.284), channel_id=1, source_target_pairs={{0,8},{4,12},{8,0},{12,4},{16,24},{20,28},{24,16},{28,20},{1,9},{5... | collective-permute-start | bytes 196616 | tf_op jit(solution)/shard_map/ppermute | solution.py:407
  162.3 5.7 %collective-permute-start.83 = (f32[72,128]{1,0:T(8,128)S(1)}, f32[72,128]{1,0:T(8,128)S(1)}, u32[]{:S(2)}, u32[]{:S(2)}) collective-permute-start(f32[72,128]{1,0:T(8,128)S(1)} %add_add_fusion.4), channel_id=1, source_target_pairs={{0,1},{1,0},{2,3},{3,2},{4,5},{5,4},{6,7},{7,6},{8,9},{9,8},{10,11... | collective-permute-start | bytes 110600 | tf_op jit(solution)/shard_map/ppermute | solution.py:407
  164.2 4.7 %collective-permute-start.74 = (bf16[256,128]{1,0:T(8,128)(2,1)S(1)}, bf16[256,128]{1,0:T(8,128)(2,1)S(1)}, u32[]{:S(2)}, u32[]{:S(2)}) collective-permute-start(bf16[256,128]{1,0:T(8,128)(2,1)S(1)} %get-tuple-element.285), channel_id=1, source_target_pairs={{0,12},{4,8},{8,4},{12,0},{16,28},{20,24},{24,20},{28,16},{1,13},{... | collective-permute-start | bytes 196616 | tf_op jit(solution)/shard_map/ppermute | solution.py:407
  164.6 6.0 %collective-permute-start.75 = (bf16[256,128]{1,0:T(8,128)(2,1)S(1)}, bf16[256,128]{1,0:T(8,128)(2,1)S(1)}, u32[]{:S(2)}, u32[]{:S(2)}) collective-permute-start(bf16[256,128]{1,0:T(8,128)(2,1)S(1)} %get-tuple-element.286), channel_id=1, source_target_pairs={{0,16},{4,20},{8,24},{12,28},{16,0},{20,4},{24,8},{28,12},{1,17},{... | collective-permute-start | bytes 196616 | tf_op jit(solution)/shard_map/ppermute | solution.py:407
  166.2 6.4 %collective-permute-start.76 = (bf16[256,128]{1,0:T(8,128)(2,1)S(1)}, bf16[256,128]{1,0:T(8,128)(2,1)S(1)}, u32[]{:S(2)}, u32[]{:S(2)}) collective-permute-start(bf16[256,128]{1,0:T(8,128)(2,1)S(1)} %get-tuple-element.287), channel_id=1, source_target_pairs={{0,20},{4,16},{8,28},{12,24},{16,4},{20,0},{24,12},{28,8},{1,21},{... | collective-permute-start | bytes 196616 | tf_op jit(solution)/shard_map/ppermute | solution.py:407
  166.5 6.1 %collective-permute-start.77 = (bf16[256,128]{1,0:T(8,128)(2,1)S(1)}, bf16[256,128]{1,0:T(8,128)(2,1)S(1)}, u32[]{:S(2)}, u32[]{:S(2)}) collective-permute-start(bf16[256,128]{1,0:T(8,128)(2,1)S(1)} %get-tuple-element.288), channel_id=1, source_target_pairs={{0,24},{4,28},{8,16},{12,20},{16,8},{20,12},{24,0},{28,4},{1,25},{... | collective-permute-start | bytes 196616 | tf_op jit(solution)/shard_map/ppermute | solution.py:407
  168.0 5.1 %collective-permute-start.78 = (bf16[256,128]{1,0:T(8,128)(2,1)S(1)}, bf16[256,128]{1,0:T(8,128)(2,1)S(1)}, u32[]{:S(2)}, u32[]{:S(2)}) collective-permute-start(bf16[256,128]{1,0:T(8,128)(2,1)S(1)} %get-tuple-element.289), channel_id=1, source_target_pairs={{0,28},{4,24},{8,20},{12,16},{16,12},{20,8},{24,4},{28,0},{1,29},{... | collective-permute-start | bytes 196616 | tf_op jit(solution)/shard_map/ppermute | solution.py:407
  169.0 6.8 %collective-permute-start.84 = (f32[72,128]{1,0:T(8,128)S(1)}, f32[72,128]{1,0:T(8,128)S(1)}, u32[]{:S(2)}, u32[]{:S(2)}) collective-permute-start(f32[72,128]{1,0:T(8,128)S(1)} %add.123.refs_0_), channel_id=1, source_target_pairs={{0,2},{1,3},{2,0},{3,1},{4,6},{5,7},{6,4},{7,5},{8,10},{9,11},{10,... | collective-permute-start | bytes 110600 | tf_op jit(solution)/shard_map/ppermute | solution.py:407
  175.5 8.6 %collective-permute-start.92 = (f32[72,128]{1,0:T(8,128)S(1)}, f32[72,128]{1,0:T(8,128)S(1)}, u32[]{:S(2)}, u32[]{:S(2)}) collective-permute-start(f32[72,128]{1,0:T(8,128)S(1)} %get-tuple-element.303), channel_id=1, source_target_pairs={{0,4},{4,0},{8,12},{12,8},{16,20},{20,16},{24,28},{28,24},{1,5},{5... | collective-permute-start | bytes 110600 | tf_op jit(solution)/shard_map/ppermute | solution.py:407
  181.9 9.3 %collective-permute-start.85 = (bf16[256,128]{1,0:T(8,128)(2,1)S(1)}, bf16[256,128]{1,0:T(8,128)(2,1)S(1)}, u32[]{:S(2)}, u32[]{:S(2)}) collective-permute-start(bf16[256,128]{1,0:T(8,128)(2,1)S(1)} %get-tuple-element.295), channel_id=1, source_target_pairs={{0,4},{4,0},{8,12},{12,8},{16,20},{20,16},{24,28},{28,24},{1,5},{5... | collective-permute-start | bytes 196616 | tf_op jit(solution)/shard_map/ppermute | solution.py:407
  182.3 10.7 %collective-permute-start.86 = (bf16[256,128]{1,0:T(8,128)(2,1)S(1)}, bf16[256,128]{1,0:T(8,128)(2,1)S(1)}, u32[]{:S(2)}, u32[]{:S(2)}) collective-permute-start(bf16[256,128]{1,0:T(8,128)(2,1)S(1)} %get-tuple-element.296), channel_id=1, source_target_pairs={{0,8},{4,12},{8,0},{12,4},{16,24},{20,28},{24,16},{28,20},{1,9},{5... | collective-permute-start | bytes 196616 | tf_op jit(solution)/shard_map/ppermute | solution.py:407
  184.1 5.1 %collective-permute-start.95 = (f32[72,128]{1,0:T(8,128)S(1)}, f32[72,128]{1,0:T(8,128)S(1)}, u32[]{:S(2)}, u32[]{:S(2)}) collective-permute-start(f32[72,128]{1,0:T(8,128)S(1)} %add.124), channel_id=1, source_target_pairs={{0,24},{4,28},{8,16},{12,20},{16,8},{20,12},{24,0},{28,4},{1,25},{... | collective-permute-start | bytes 110600 | tf_op jit(solution)/shard_map/ppermute | solution.py:407
  189.2 5.1 %collective-permute-start.87 = (bf16[256,128]{1,0:T(8,128)(2,1)S(1)}, bf16[256,128]{1,0:T(8,128)(2,1)S(1)}, u32[]{:S(2)}, u32[]{:S(2)}) collective-permute-start(bf16[256,128]{1,0:T(8,128)(2,1)S(1)} %get-tuple-element.297), channel_id=1, source_target_pairs={{0,12},{4,8},{8,4},{12,0},{16,28},{20,24},{24,20},{28,16},{1,13},{... | collective-permute-start | bytes 196616 | tf_op jit(solution)/shard_map/ppermute | solution.py:407
  189.5 5.8 %collective-permute-start.88 = (bf16[256,128]{1,0:T(8,128)(2,1)S(1)}, bf16[256,128]{1,0:T(8,128)(2,1)S(1)}, u32[]{:S(2)}, u32[]{:S(2)}) collective-permute-start(bf16[256,128]{1,0:T(8,128)(2,1)S(1)} %get-tuple-element.298), channel_id=1, source_target_pairs={{0,16},{4,20},{8,24},{12,28},{16,0},{20,4},{24,8},{28,12},{1,17},{... | collective-permute-start | bytes 196616 | tf_op jit(solution)/shard_map/ppermute | solution.py:407
  189.9 5.4 %collective-permute-start.89 = (bf16[256,128]{1,0:T(8,128)(2,1)S(1)}, bf16[256,128]{1,0:T(8,128)(2,1)S(1)}, u32[]{:S(2)}, u32[]{:S(2)}) collective-permute-start(bf16[256,128]{1,0:T(8,128)(2,1)S(1)} %get-tuple-element.299), channel_id=1, source_target_pairs={{0,20},{4,16},{8,28},{12,24},{16,4},{20,0},{24,12},{28,8},{1,21},{... | collective-permute-start | bytes 196616 | tf_op jit(solution)/shard_map/ppermute | solution.py:407
  191.2 5.8 %collective-permute-start.90 = (bf16[256,128]{1,0:T(8,128)(2,1)S(1)}, bf16[256,128]{1,0:T(8,128)(2,1)S(1)}, u32[]{:S(2)}, u32[]{:S(2)}) collective-permute-start(bf16[256,128]{1,0:T(8,128)(2,1)S(1)} %get-tuple-element.300), channel_id=1, source_target_pairs={{0,24},{4,28},{8,16},{12,20},{16,8},{20,12},{24,0},{28,4},{1,25},{... | collective-permute-start | bytes 196616 | tf_op jit(solution)/shard_map/ppermute | solution.py:407
  193.0 4.9 %collective-permute-start.91 = (bf16[256,128]{1,0:T(8,128)(2,1)S(1)}, bf16[256,128]{1,0:T(8,128)(2,1)S(1)}, u32[]{:S(2)}, u32[]{:S(2)}) collective-permute-start(bf16[256,128]{1,0:T(8,128)(2,1)S(1)} %get-tuple-element.301), channel_id=1, source_target_pairs={{0,28},{4,24},{8,20},{12,16},{16,12},{20,8},{24,4},{28,0},{1,29},{... | collective-permute-start | bytes 196616 | tf_op jit(solution)/shard_map/ppermute | solution.py:407
  194.3 6.3 %collective-permute-start.96 = (f32[72,128]{1,0:T(8,128)S(1)}, f32[72,128]{1,0:T(8,128)S(1)}, u32[]{:S(2)}, u32[]{:S(2)}) collective-permute-start(f32[72,128]{1,0:T(8,128)S(1)} %add_add_fusion.3), channel_id=1, source_target_pairs={{0,1},{1,0},{2,3},{3,2},{4,5},{5,4},{6,7},{7,6},{8,9},{9,8},{10,11... | collective-permute-start | bytes 110600 | tf_op jit(solution)/shard_map/ppermute | solution.py:407
  200.7 5.4 %collective-permute-start.97 = (f32[72,128]{1,0:T(8,128)S(1)}, f32[72,128]{1,0:T(8,128)S(1)}, u32[]{:S(2)}, u32[]{:S(2)}) collective-permute-start(f32[72,128]{1,0:T(8,128)S(1)} %add.128.refs_0_), channel_id=1, source_target_pairs={{0,2},{1,3},{2,0},{3,1},{4,6},{5,7},{6,4},{7,5},{8,10},{9,11},{10,... | collective-permute-start | bytes 110600 | tf_op jit(solution)/shard_map/ppermute | solution.py:407
  202.3 11.6 %collective-permute-start.108 = (f32[72,128]{1,0:T(8,128)S(1)}, f32[72,128]{1,0:T(8,128)S(1)}, u32[]{:S(2)}, u32[]{:S(2)}) collective-permute-start(f32[72,128]{1,0:T(8,128)S(1)} %add.130), channel_id=1, source_target_pairs={{0,24},{4,28},{8,16},{12,20},{16,8},{20,12},{24,0},{28,4},{1,25},{... | collective-permute-start | bytes 110600 | tf_op jit(solution)/shard_map/ppermute | solution.py:407
  204.0 9.9 %collective-permute-start.107 = (f32[72,128]{1,0:T(8,128)S(1)}, f32[72,128]{1,0:T(8,128)S(1)}, u32[]{:S(2)}, u32[]{:S(2)}) collective-permute-start(f32[72,128]{1,0:T(8,128)S(1)} %add.130), channel_id=1, source_target_pairs={{0,16},{4,20},{8,24},{12,28},{16,0},{20,4},{24,8},{28,12},{1,17},{... | collective-permute-start | bytes 110600 | tf_op jit(solution)/shard_map/ppermute | solution.py:407
  205.2 8.7 %collective-permute-start.106 = (f32[72,128]{1,0:T(8,128)S(1)}, f32[72,128]{1,0:T(8,128)S(1)}, u32[]{:S(2)}, u32[]{:S(2)}) collective-permute-start(f32[72,128]{1,0:T(8,128)S(1)} %add.130), channel_id=1, source_target_pairs={{0,8},{4,12},{8,0},{12,4},{16,24},{20,28},{24,16},{28,20},{1,9},{5... | collective-permute-start | bytes 110600 | tf_op jit(solution)/shard_map/ppermute | solution.py:407
  213.9 4.7 %collective-permute-start.109 = (f32[72,128]{1,0:T(8,128)S(1)}, f32[72,128]{1,0:T(8,128)S(1)}, u32[]{:S(2)}, u32[]{:S(2)}) collective-permute-start(f32[72,128]{1,0:T(8,128)S(1)} %add_add_fusion.2), channel_id=1, source_target_pairs={{0,1},{1,0},{2,3},{3,2},{4,5},{5,4},{6,7},{7,6},{8,9},{9,8},{10,11... | collective-permute-start | bytes 110600 | tf_op jit(solution)/shard_map/ppermute | solution.py:407
  214.5 4.8 %collective-permute-start.100 = (bf16[256,128]{1,0:T(8,128)(2,1)S(1)}, bf16[256,128]{1,0:T(8,128)(2,1)S(1)}, u32[]{:S(2)}, u32[]{:S(2)}) collective-permute-start(bf16[256,128]{1,0:T(8,128)(2,1)S(1)} %get-tuple-element.310), channel_id=1, source_target_pairs={{0,12},{4,8},{8,4},{12,0},{16,28},{20,24},{24,20},{28,16},{1,13},{... | collective-permute-start | bytes 196616 | tf_op jit(solution)/shard_map/ppermute | solution.py:407
  214.9 6.3 %collective-permute-start.101 = (bf16[256,128]{1,0:T(8,128)(2,1)S(1)}, bf16[256,128]{1,0:T(8,128)(2,1)S(1)}, u32[]{:S(2)}, u32[]{:S(2)}) collective-permute-start(bf16[256,128]{1,0:T(8,128)(2,1)S(1)} %get-tuple-element.311), channel_id=1, source_target_pairs={{0,16},{4,20},{8,24},{12,28},{16,0},{20,4},{24,8},{28,12},{1,17},{... | collective-permute-start | bytes 196616 | tf_op jit(solution)/shard_map/ppermute | solution.py:407
  216.3 4.9 %collective-permute-start.102 = (bf16[256,128]{1,0:T(8,128)(2,1)S(1)}, bf16[256,128]{1,0:T(8,128)(2,1)S(1)}, u32[]{:S(2)}, u32[]{:S(2)}) collective-permute-start(bf16[256,128]{1,0:T(8,128)(2,1)S(1)} %get-tuple-element.312), channel_id=1, source_target_pairs={{0,20},{4,16},{8,28},{12,24},{16,4},{20,0},{24,12},{28,8},{1,21},{... | collective-permute-start | bytes 196616 | tf_op jit(solution)/shard_map/ppermute | solution.py:407
  216.9 5.2 %collective-permute-start.103 = (bf16[256,128]{1,0:T(8,128)(2,1)S(1)}, bf16[256,128]{1,0:T(8,128)(2,1)S(1)}, u32[]{:S(2)}, u32[]{:S(2)}) collective-permute-start(bf16[256,128]{1,0:T(8,128)(2,1)S(1)} %get-tuple-element.313), channel_id=1, source_target_pairs={{0,24},{4,28},{8,16},{12,20},{16,8},{20,12},{24,0},{28,4},{1,25},{... | collective-permute-start | bytes 196616 | tf_op jit(solution)/shard_map/ppermute | solution.py:407
  218.7 5.1 %collective-permute-start.104 = (bf16[256,128]{1,0:T(8,128)(2,1)S(1)}, bf16[256,128]{1,0:T(8,128)(2,1)S(1)}, u32[]{:S(2)}, u32[]{:S(2)}) collective-permute-start(bf16[256,128]{1,0:T(8,128)(2,1)S(1)} %get-tuple-element.314), channel_id=1, source_target_pairs={{0,28},{4,24},{8,20},{12,16},{16,12},{20,8},{24,4},{28,0},{1,29},{... | collective-permute-start | bytes 196616 | tf_op jit(solution)/shard_map/ppermute | solution.py:407
  219.3 6.4 %collective-permute-start.110 = (f32[72,128]{1,0:T(8,128)S(1)}, f32[72,128]{1,0:T(8,128)S(1)}, u32[]{:S(2)}, u32[]{:S(2)}) collective-permute-start(f32[72,128]{1,0:T(8,128)S(1)} %add.134.refs_0_), channel_id=1, source_target_pairs={{0,2},{1,3},{2,0},{3,1},{4,6},{5,7},{6,4},{7,5},{8,10},{9,11},{10,... | collective-permute-start | bytes 110600 | tf_op jit(solution)/shard_map/ppermute | solution.py:407
  233.8 4.9 %collective-permute-start.114 = (f32[72,128]{1,0:T(8,128)S(1)}, f32[72,128]{1,0:T(8,128)S(1)}, u32[]{:S(2)}, u32[]{:S(2)}) collective-permute-start(f32[72,128]{1,0:T(8,128)S(1)} %add.135), channel_id=1, source_target_pairs={{0,24},{4,28},{8,16},{12,20},{16,8},{20,12},{24,0},{28,4},{1,25},{... | collective-permute-start | bytes 110600 | tf_op jit(solution)/shard_map/ppermute | solution.py:407
  240.6 6.9 %collective-permute-start.117 = (f32[72,128]{1,0:T(8,128)S(1)}, f32[72,128]{1,0:T(8,128)S(1)}, u32[]{:S(2)}, u32[]{:S(2)}) collective-permute-start(f32[72,128]{1,0:T(8,128)S(1)} %add_add_fusion.1.refs_0_), channel_id=1, source_target_pairs={{0,3},{1,2},{2,1},{3,0},{4,7},{5,6},{6,5},{7,4},{8,11},{9,10},{10,... | collective-permute-start | bytes 110600 | tf_op jit(solution)/shard_map/ppermute | solution.py:407
  242.8 5.0 %collective-permute-start.116 = (f32[72,128]{1,0:T(8,128)S(1)}, f32[72,128]{1,0:T(8,128)S(1)}, u32[]{:S(2)}, u32[]{:S(2)}) collective-permute-start(f32[72,128]{1,0:T(8,128)S(1)} %add_add_fusion.1.refs_0_), channel_id=1, source_target_pairs={{0,2},{1,3},{2,0},{3,1},{4,6},{5,7},{6,4},{7,5},{8,10},{9,11},{10,... | collective-permute-start | bytes 110600 | tf_op jit(solution)/shard_map/ppermute | solution.py:407
  (34 other events, 323.0 us)
